TPU v7x, 256 devices: a whole 4x4x8 slice. The times are simulated.
256 devices in a mesh: chan: 128 (over x, y, z), tm: 2 (over core).
Axes of the slice: x: 4, y: 4, z: 8, core: 2. Of those that a mesh axis runs over, the one named last changes fastest.
Arguments:
- traces: bfloat16 [2, 128, 128, 1536], P('tm', 'chan'), may hold values from -2.5 to 2.5
- pair_target: int32 [128, 3], P('chan'), may hold values from 1 to 127, as said below
- pair_count: int32 [128], P('chan'), may hold values from 0 to 3, as said below
Outputs:
- stacked: float32 [128, 3, 33, 128, 128], P('chan', None, None, 'tm')
Inputs may be any that keep to these rules, and one draw needn't show every extreme that they name: For j < pair_count[b], the entries pair_target[b, j] are distinct blocks among b + 1 .. b + 7; later slots hold arbitrary blocks above b, or b itself for the last block. pair_count[b] is at most the number of blocks after b; the last block has none.
All inputs are finite; a program needn't handle non-finite values.
Results may differ from a plain program's by a relative error of at most 0.0003.
Values may be sent and summed in bfloat16 or wider, within the bound.
No kernel may reach another device: no remote copies, remote signals or barrier semaphores. Data moves between devices by JAX's collectives and lax.ppermute only.
A program may use at most 128 MiB of HBM per device.

v0:
```python
import jax
import jax.numpy as jnp
from jax import lax
from jax.sharding import PartitionSpec as P

MAXLAG = 16
REACH = 7
P_MAX = 3


def passed_along(block, axis, distance):
    devices = range(lax.axis_size(axis))
    route = [(i - distance, i) for i in devices if i - distance in devices]
    return lax.ppermute(block, axis, route)


def correlate(source, target):
    lag_total = 2 * MAXLAG + 1
    samples = source.shape[1]
    padded = jnp.pad(target, ((0, 0), (MAXLAG, MAXLAG)))
    pieces = []
    for lag_start in range(0, lag_total, 11):
        shifted = jnp.stack(
            [
                padded[:, lag_index : lag_index + samples]
                for lag_index in range(lag_start, min(lag_start + 11, lag_total))
            ]
        )
        pieces.append(
            jnp.einsum("it,lkt->lik", source, shifted, preferred_element_type=jnp.float32)
        )
    return jnp.concatenate(pieces, 0)


def body(traces, pair_target, pair_count):
    own_block = traces[0, 0]
    my_index = lax.axis_index("chan")
    slot_count = pair_count[0]
    offsets = jnp.clip(pair_target[0] - my_index, 1, REACH)

    def advance(carry, unused):
        moved = passed_along(carry, "chan", -1)
        return (moved, moved)

    _, window = lax.scan(advance, own_block, None, length=REACH)
    selected = jnp.take(window, offsets - 1, axis=0)

    def one_tile(source, target, slot_id):
        return correlate(source, target) * (slot_id < slot_count).astype(jnp.float32)

    tile_stack = jnp.stack(
        [one_tile(own_block, selected[slot_id], slot_id) for slot_id in range(P_MAX)]
    )
    result = lax.psum_scatter(tile_stack, "tm", scatter_dimension=2, tiled=True)
    return result[None]


def solution(mesh):
    placed = (P("tm", "chan", None, None), P("chan", None), P("chan"))
    return jax.shard_map(
        body,
        mesh=mesh,
        in_specs=placed,
        out_specs=P("chan", None, None, "tm", None),
        check_vma=False,
    )
```

profile of v0, /device:TPU:1, one launch (start us, length us, event | category | flops | bytes accessed | tf_op | source)
XLA Modules:
  0.0 198.1 jit_solution(387866569733338073)
XLA Ops:
  9.5 80.4 %while.12 = (s32[]{:T(128)}, bf16[128,1536]{1,0:T(8,128)(2,1)S(1)}, bf16[7,128,1536]{2,1,0:T(8,128)(2,1)}, s32[]{:T(128)}) while((s32[]{:T(128)}, bf16[128,1536]{1,0:T(8,128)(2,1)S(1)}, bf16[7,128,1536]{2,1,0:T(8,128)(2,1)}, s32[]{:T(128)}) %tuple.32), condition=%wide.region_1.2_spmd, body=%wide.region_0.1_spmd.sunk | while | flops 2 | bytes 3145833 | solution.py:45
  9.5 1.3 collective-permute-start
  10.8 10.0 %collective-permute-done = bf16[128,1536]{1,0:T(8,128)(2,1)S(1)} collective-permute-done((bf16[128,1536]{1,0:T(8,128)(2,1)S(1)}, bf16[128,1536]{1,0:T(8,128)(2,1)S(1)}, u32[]{:S(2)}, u32[]{:S(2)}) %collective-permute-start) | collective-permute-done | bytes 393248 | tf_op jit(solution)/shard_map/while/body/eval_jaxpr/ppermute | solution.py:14
  21.6 1.3 collective-permute-start
  22.9 12.0 %collective-permute-done = bf16[128,1536]{1,0:T(8,128)(2,1)S(1)} collective-permute-done((bf16[128,1536]{1,0:T(8,128)(2,1)S(1)}, bf16[128,1536]{1,0:T(8,128)(2,1)S(1)}, u32[]{:S(2)}, u32[]{:S(2)}) %collective-permute-start) | collective-permute-done | bytes 393248 | tf_op jit(solution)/shard_map/while/body/eval_jaxpr/ppermute | solution.py:14
  37.0 9.5 %collective-permute-done = bf16[128,1536]{1,0:T(8,128)(2,1)S(1)} collective-permute-done((bf16[128,1536]{1,0:T(8,128)(2,1)S(1)}, bf16[128,1536]{1,0:T(8,128)(2,1)S(1)}, u32[]{:S(2)}, u32[]{:S(2)}) %collective-permute-start) | collective-permute-done | bytes 393248 | tf_op jit(solution)/shard_map/while/body/eval_jaxpr/ppermute | solution.py:14
  48.6 10.6 %collective-permute-done = bf16[128,1536]{1,0:T(8,128)(2,1)S(1)} collective-permute-done((bf16[128,1536]{1,0:T(8,128)(2,1)S(1)}, bf16[128,1536]{1,0:T(8,128)(2,1)S(1)}, u32[]{:S(2)}, u32[]{:S(2)}) %collective-permute-start) | collective-permute-done | bytes 393248 | tf_op jit(solution)/shard_map/while/body/eval_jaxpr/ppermute | solution.py:14
  61.3 8.3 %collective-permute-done = bf16[128,1536]{1,0:T(8,128)(2,1)S(1)} collective-permute-done((bf16[128,1536]{1,0:T(8,128)(2,1)S(1)}, bf16[128,1536]{1,0:T(8,128)(2,1)S(1)}, u32[]{:S(2)}, u32[]{:S(2)}) %collective-permute-start) | collective-permute-done | bytes 393248 | tf_op jit(solution)/shard_map/while/body/eval_jaxpr/ppermute | solution.py:14
  71.7 7.6 %collective-permute-done = bf16[128,1536]{1,0:T(8,128)(2,1)S(1)} collective-permute-done((bf16[128,1536]{1,0:T(8,128)(2,1)S(1)}, bf16[128,1536]{1,0:T(8,128)(2,1)S(1)}, u32[]{:S(2)}, u32[]{:S(2)}) %collective-permute-start) | collective-permute-done | bytes 393248 | tf_op jit(solution)/shard_map/while/body/eval_jaxpr/ppermute | solution.py:14
  81.4 7.7 %collective-permute-done = bf16[128,1536]{1,0:T(8,128)(2,1)S(1)} collective-permute-done((bf16[128,1536]{1,0:T(8,128)(2,1)S(1)}, bf16[128,1536]{1,0:T(8,128)(2,1)S(1)}, u32[]{:S(2)}, u32[]{:S(2)}) %collective-permute-start) | collective-permute-done | bytes 393248 | tf_op jit(solution)/shard_map/while/body/eval_jaxpr/ppermute | solution.py:14
  89.9 2.4 %gather_fusion = bf16[3,128,1536]{2,1,0:T(8,128)(2,1)S(1)} fusion(bf16[7,128,1536]{2,1,0:T(8,128)(2,1)} %get-tuple-element.22, s32[1024]{0:T(1024)S(1)} %pad_clamp_fusion), kind=kCustom, calls=%fused_computation | custom fusion | bytes 2359308 | tf_op jit(solution)/shard_map/jit(_take)/gather | solution.py:46
  98.3 1.3 convolution_bitcast_fusion.5
  100.7 1.3 convolution_bitcast_fusion.2
  103.1 1.3 convolution_bitcast_fusion.8
  106.2 1.5 convolution_bitcast_fusion.7
  109.3 1.3 convolution_bitcast_fusion.6
  111.6 1.3 convolution_bitcast_fusion.4
  115.3 1.3 convolution_bitcast_fusion.1
  118.3 1.3 convolution_bitcast_fusion
  119.6 1.3 convolution_bitcast_fusion.3
  121.4 3.4 %pad_maximum_fusion = f32[3,33,128,128]{2,3,1,0:T(8,128)} fusion(f32[1,33,128,128]{2,3,1,0:T(8,128)S(1)} %maximum_multiply_fusion.2, f32[1,33,128,128]{2,3,1,0:T(8,128)S(1)} %maximum_multiply_fusion.1, f32[1,33,128,128]{2,3,1,0:T(8,128)S(1)} %maximum_multiply_fusion), kind=kLoop, calls=%fused_computation.2 | loop fusion | flops 3244032 | bytes 12976128 | tf_op jit(solution)/shard_map/stack | solution.py:51
  124.8 7.9 %copy.5 = f32[3,33,128,128]{3,1,0,2:T(8,128)} copy(f32[3,33,128,128]{2,3,1,0:T(8,128)} %pad_maximum_fusion) | data formatting | bytes 12976128 | tf_op jit(solution)/shard_map/stack | solution.py:51
  132.7 54.2 %reduce-scatter.2.cloned.1.call-done = f32[3,33,64,128]{3,1,0,2:T(8,128)} async-done(((f32[3,33,128,128]{3,1,0,2:T(8,128)}), f32[3,33,64,128]{3,1,0,2:T(8,128)}) %reduce-scatter.2.cloned.1.call-update) | async-done | bytes 3244048 | tf_op jit(solution)/shard_map/reduce_scatter | solution.py:54
  186.9 4.4 %copy.6 = f32[1,3,33,64,128]{4,3,2,1,0:T(8,128)} copy(f32[1,3,33,64,128]{4,2,1,3,0:T(8,128)} %bitcast.283) | data formatting | bytes 6488064 | tf_op jit(solution)/shard_map/broadcast_in_dim | solution.py:55
  (120 shorter events, 31.3 us)
Async XLA Ops:
  6.5 180.4 %reduce-scatter.2.cloned.1.call-start = ((), (), s32[]{:S(2)}) async-start(), calls=%async_computation.1 | async-start | bytes 11796480 | tf_op jit(solution)/shard_map/reduce_scatter | solution.py:54
  9.5 11.3 %collective-permute-start = (bf16[128,1536]{1,0:T(8,128)(2,1)S(1)}, bf16[128,1536]{1,0:T(8,128)(2,1)S(1)}, u32[]{:S(2)}, u32[]{:S(2)}) collective-permute-start(bf16[128,1536]{1,0:T(8,128)(2,1)S(1)} %get-tuple-element.76), channel_id=1, source_target_pairs={{2,0},{4,2},{6,4},{8,6},{10,8},{12,10},{14,12},{16,14},{18,16},{20... | collective-permute-start | bytes 1179656 | tf_op jit(solution)/shard_map/while/body/eval_jaxpr/ppermute | solution.py:14
  21.6 13.3 %collective-permute-start = (bf16[128,1536]{1,0:T(8,128)(2,1)S(1)}, bf16[128,1536]{1,0:T(8,128)(2,1)S(1)}, u32[]{:S(2)}, u32[]{:S(2)}) collective-permute-start(bf16[128,1536]{1,0:T(8,128)(2,1)S(1)} %get-tuple-element.76), channel_id=1, source_target_pairs={{2,0},{4,2},{6,4},{8,6},{10,8},{12,10},{14,12},{16,14},{18,16},{20... | collective-permute-start | bytes 1179656 | tf_op jit(solution)/shard_map/while/body/eval_jaxpr/ppermute | solution.py:14
  35.8 10.8 %collective-permute-start = (bf16[128,1536]{1,0:T(8,128)(2,1)S(1)}, bf16[128,1536]{1,0:T(8,128)(2,1)S(1)}, u32[]{:S(2)}, u32[]{:S(2)}) collective-permute-start(bf16[128,1536]{1,0:T(8,128)(2,1)S(1)} %get-tuple-element.76), channel_id=1, source_target_pairs={{2,0},{4,2},{6,4},{8,6},{10,8},{12,10},{14,12},{16,14},{18,16},{20... | collective-permute-start | bytes 1179656 | tf_op jit(solution)/shard_map/while/body/eval_jaxpr/ppermute | solution.py:14
  47.3 11.8 %collective-permute-start = (bf16[128,1536]{1,0:T(8,128)(2,1)S(1)}, bf16[128,1536]{1,0:T(8,128)(2,1)S(1)}, u32[]{:S(2)}, u32[]{:S(2)}) collective-permute-start(bf16[128,1536]{1,0:T(8,128)(2,1)S(1)} %get-tuple-element.76), channel_id=1, source_target_pairs={{2,0},{4,2},{6,4},{8,6},{10,8},{12,10},{14,12},{16,14},{18,16},{20... | collective-permute-start | bytes 1179656 | tf_op jit(solution)/shard_map/while/body/eval_jaxpr/ppermute | solution.py:14
  60.0 9.6 %collective-permute-start = (bf16[128,1536]{1,0:T(8,128)(2,1)S(1)}, bf16[128,1536]{1,0:T(8,128)(2,1)S(1)}, u32[]{:S(2)}, u32[]{:S(2)}) collective-permute-start(bf16[128,1536]{1,0:T(8,128)(2,1)S(1)} %get-tuple-element.76), channel_id=1, source_target_pairs={{2,0},{4,2},{6,4},{8,6},{10,8},{12,10},{14,12},{16,14},{18,16},{20... | collective-permute-start | bytes 1179656 | tf_op jit(solution)/shard_map/while/body/eval_jaxpr/ppermute | solution.py:14
  70.4 8.9 %collective-permute-start = (bf16[128,1536]{1,0:T(8,128)(2,1)S(1)}, bf16[128,1536]{1,0:T(8,128)(2,1)S(1)}, u32[]{:S(2)}, u32[]{:S(2)}) collective-permute-start(bf16[128,1536]{1,0:T(8,128)(2,1)S(1)} %get-tuple-element.76), channel_id=1, source_target_pairs={{2,0},{4,2},{6,4},{8,6},{10,8},{12,10},{14,12},{16,14},{18,16},{20... | collective-permute-start | bytes 1179656 | tf_op jit(solution)/shard_map/while/body/eval_jaxpr/ppermute | solution.py:14
  80.1 9.0 %collective-permute-start = (bf16[128,1536]{1,0:T(8,128)(2,1)S(1)}, bf16[128,1536]{1,0:T(8,128)(2,1)S(1)}, u32[]{:S(2)}, u32[]{:S(2)}) collective-permute-start(bf16[128,1536]{1,0:T(8,128)(2,1)S(1)} %get-tuple-element.76), channel_id=1, source_target_pairs={{2,0},{4,2},{6,4},{8,6},{10,8},{12,10},{14,12},{16,14},{18,16},{20... | collective-permute-start | bytes 1179656 | tf_op jit(solution)/shard_map/while/body/eval_jaxpr/ppermute | solution.py:14
  96.3 2.0 %copy-start = (bf16[1,1,128,1536]{3,2,1,0:T(8,128)(2,1)S(1)}, bf16[1,1,128,1536]{3,2,1,0:T(8,128)(2,1)}, u32[]{:S(2)}) copy-start(bf16[1,1,128,1536]{3,2,1,0:T(8,128)(2,1)} %param.5) | copy-start | bytes 1179652
Sparse Core Ops, SparseCore 0:
  132.8 54.0 reduce-scatter.1
where the time goes:
time: 199 us; the launch traced here: 198 us
  waiting for transfers between devices  120 us (60%)
  local copies, waits for them, and re-layouts  37.5 us (19%)
  between operations  14.5 us (7%)
  matrix products  11.8 us (6%)
  starting transfers between devices  8.96 us (5%)
  other arithmetic  5.38 us (3%)
    ppermute x7, waiting for transfers between devices, passed_along(): return lax.ppermute(block, axis, route)  65.7 us
    reduce_scatter x1, waiting for transfers between devices, body(): result = lax.psum_scatter(tile_stack, 'tm', scatter_dimension=2, tiled=True)  54.2 us
    unnamed x82, local copies, waits for them, and re-layouts  14.7 us
    dot_general x9, matrix products, correlate(): jnp.einsum('it,lkt->lik', source, shifted, preferred_element_type=jnp.flo...  11.8 us
    ppermute x7, starting transfers between devices, passed_along(): return lax.ppermute(block, axis, route)  8.96 us
    another operation x1, local copies, waits for them, and re-layouts, body(): jnp.stack([one_tile(own_block, selected[slot_id], slot_id) for slot_id in...  7.89 us
    dynamic_update_slice x7, local copies, waits for them, and re-layouts, body(): _, window = lax.scan(advance, own_block, None, length=REACH)  5.44 us
    broadcast_in_dim x1, local copies, waits for them, and re-layouts, body(): return result[None]  4.37 us
  transfers between devices with their start and end apart: 8, of which 8 were waited for; matrix products, arithmetic and copies ran while one was open for 0% of the time, Pallas kernels for 0%

commit v1 on v0

v1 whole, which is shorter than its diff:
```python
import functools

import jax
import jax.numpy as jnp
from jax import lax
from jax.experimental import pallas as pl
from jax.experimental.pallas import tpu as pltpu
from jax.sharding import PartitionSpec as P

MAXLAG = 16
REACH = 7
P_MAX = 3
LAGS = 2 * MAXLAG + 1
PAIRS = MAXLAG + 1
EDGE = 128
VMEM = pl.BlockSpec(memory_space=pltpu.VMEM)
SMEM = pl.BlockSpec(memory_space=pltpu.SMEM)
ANY = pl.BlockSpec(memory_space=pl.ANY)
CHUNKS = ((0, 4), (4, 8), (8, 12), (12, 17))


def stack_kernel(first, second, out, padded):
    half, samples = first.shape
    padded[...] = jnp.zeros_like(padded)
    for g, source in enumerate((first, second)):
        padded[:, EDGE : EDGE + samples] = source[...]
        for m in range(PAIRS):
            start = EDGE + MAXLAG - 2 * m
            out[m * half : (m + 1) * half, g * samples : (g + 1) * samples] = padded[:, start : start + samples]
    lane = lax.broadcasted_iota(jnp.int32, (half, EDGE), 1)
    for m in range(PAIRS):
        at = MAXLAG - 1 - 2 * m
        edge = jnp.zeros((half, EDGE), jnp.float32)
        if at >= 0:
            for g, source in enumerate((first, second)):
                column = source[:, :EDGE].astype(jnp.float32)[:, at : at + 1]
                edge = jnp.where(lane == g, column, edge)
        out[m * half : (m + 1) * half, 2 * samples :] = edge.astype(jnp.bfloat16)


def stack(first, second):
    half, samples = first.shape
    return pl.pallas_call(
        stack_kernel,
        out_shape=jax.ShapeDtypeStruct((PAIRS * half, 2 * samples + EDGE), jnp.bfloat16),
        in_specs=[VMEM, VMEM],
        out_specs=VMEM,
        scratch_shapes=[pltpu.VMEM((half, samples + 2 * EDGE), jnp.bfloat16)],
        compiler_params=pltpu.CompilerParams(vmem_limit_bytes=24 * 2**20),
        name="stack",
    )(first, second)


def fill_columns(own, other, columns):
    count, samples = own.shape
    lane = lax.broadcasted_iota(jnp.int32, (count, EDGE), 1)
    edge = jnp.zeros((count, EDGE), jnp.float32)
    for g, target in enumerate((own, other)):
        block = target[...]
        columns[:count, g * samples : (g + 1) * samples] = block
        ahead = jnp.concatenate([block[:, 1:], jnp.zeros((count, 1), block.dtype)], 1)
        columns[count:, g * samples : (g + 1) * samples] = ahead
        edge = jnp.where(lane == g, block[:, :EDGE].astype(jnp.float32)[:, :1], edge)
    columns[:count, 2 * samples :] = jnp.zeros((count, EDGE), jnp.bfloat16)
    columns[count:, 2 * samples :] = edge.astype(jnp.bfloat16)


def tile_kernel(distances, first, *refs):
    n = len(distances)
    wanted, stacked = refs[0], refs[1]
    own, other = refs[2 : 2 + n], refs[2 + n : 2 + 2 * n]
    out, columns, rows, tile, row_sem, out_sem = refs[-6:]
    count = own[0].shape[0]
    half = rows.shape[0] // PAIRS

    def is_here(slot):
        here = wanted[slot] == distances[0]
        for d in distances[1:]:
            here = jnp.logical_or(here, wanted[slot] == d)
        return here

    some = jnp.logical_or(jnp.logical_or(is_here(0), is_here(1)), is_here(2))
    row_copy = pltpu.make_async_copy(stacked, rows, row_sem)

    @pl.when(some)
    def _():
        row_copy.start()

    def send(slot, c):
        low, high = CHUNKS[c]
        lags = pl.ds(2 * low, min(2 * high, LAGS) - 2 * low)
        return pltpu.make_async_copy(tile.at[lags], out.at[0, slot, lags], out_sem.at[c])

    if first:

        @pl.loop(0, P_MAX)
        def _(slot):
            @pl.when(wanted[slot] == 0)
            def _():
                tile[...] = jnp.zeros_like(tile)
                for c in range(len(CHUNKS)):
                    send(slot, c).start()
                for c in range(len(CHUNKS)):
                    send(slot, c).wait()

    @pl.when(some)
    def _():
        row_copy.wait()

    @pl.loop(0, P_MAX)
    def _(slot):
        @pl.when(is_here(slot))
        def _():
            for k, d in enumerate(distances):

                @pl.when(wanted[slot] == d)
                def _(k=k):
                    fill_columns(own[k], other[k], columns)

            for c, (low, high) in enumerate(CHUNKS):
                got = lax.dot_general(
                    rows[low * half : high * half, :],
                    columns[...],
                    (((1,), (1,)), ((), ())),
                    preferred_element_type=jnp.float32,
                )
                for m in range(low, high):
                    part = got[(m - low) * half : (m - low + 1) * half]
                    tile[2 * m] = part[:, :count]
                    if 2 * m + 1 < LAGS:
                        tile[2 * m + 1] = part[:, count:]
                send(slot, c).start()
            for c in range(len(CHUNKS)):
                send(slot, c).wait()


def tiles(distances, wanted, stacked, own, other, so_far=None):
    rows = stacked.shape
    count, samples = own[0].shape
    half = rows[0] // PAIRS
    arguments = [wanted, stacked, *own, *other]
    specs = [SMEM, ANY] + [VMEM] * (2 * len(own))
    aliases = {}
    if so_far is not None:
        aliases = {len(arguments): 0}
        arguments.append(so_far)
        specs.append(ANY)
    return pl.pallas_call(
        functools.partial(tile_kernel, distances, so_far is None),
        out_shape=jax.ShapeDtypeStruct((1, P_MAX, LAGS, half, count), jnp.float32),
        in_specs=specs,
        out_specs=ANY,
        scratch_shapes=[
            pltpu.VMEM((2 * count, rows[1]), jnp.bfloat16),
            pltpu.VMEM(rows, jnp.bfloat16),
            pltpu.VMEM((LAGS, half, count), jnp.float32),
            pltpu.SemaphoreType.DMA,
            pltpu.SemaphoreType.DMA((len(CHUNKS),)),
        ],
        input_output_aliases=aliases,
        compiler_params=pltpu.CompilerParams(vmem_limit_bytes=24 * 2**20),
        name="tiles_" + "_".join(map(str, distances)),
    )(*arguments)


def body(traces, pair_target, pair_count):
    own = traces[0, 0]
    half = own.shape[0] // 2
    blocks = lax.axis_size("chan")
    me, core = lax.axis_index("chan"), lax.axis_index("tm")
    slots = jnp.arange(P_MAX, dtype=jnp.int32)
    wanted = jnp.where(slots < pair_count[0], pair_target[0] - me, 0).astype(jnp.int32)

    row = 8
    everyone = range(blocks)
    down = [((i + 1) % blocks, i) for i in everyone]
    up = [((i - 1) % blocks, i) for i in everyone]
    next_row = [((i + row) % blocks, i) if i % row < row - 1 else (i, i) for i in everyone]
    turn = [(i - 1, i) if i % row else (i + row - 1, i) for i in everyone]

    def move(block, route):
        return lax.ppermute(block, "chan", route)

    def swap(block):
        return lax.ppermute(block, "tm", [(0, 1), (1, 0)])

    below = move(own, next_row)
    d1 = move(own, down)
    d7 = move(below, turn)
    d2 = move(d1, down)
    d6 = move(d7, up)
    d3 = move(d2, down)
    d5 = move(d6, up)
    d4 = move(d3, down)

    mine = lax.dynamic_slice_in_dim(own, core * half, half, 0)
    theirs = swap(lax.dynamic_slice_in_dim(own, (1 - core) * half, half, 0))
    rows = stack(mine, theirs)
    result = None
    for distances, held in (((1, 7), (d1, d7)), ((2, 6), (d2, d6)), ((3, 5), (d3, d5)), ((4,), (d4,))):
        result = tiles(distances, wanted, rows, held, [swap(b) for b in held], result)
    return result


def solution(mesh):
    placed = (P("tm", "chan", None, None), P("chan", None), P("chan"))
    return jax.shard_map(
        body,
        mesh=mesh,
        in_specs=placed,
        out_specs=P("chan", None, None, "tm", None),
        check_vma=False,
    )
```

time: 199 us -> 84.4 us (0.42)
  waiting for transfers between devices: 120 us -> 17.6 us
  starting transfers between devices: 8.96 us -> 47.1 us
  local copies, waits for them, and re-layouts: 37.5 us -> 1.05 us
  Pallas kernels: 0 us -> 16.7 us
  between operations: 14.5 us -> 0.91 us
  matrix products: 11.8 us -> 0 us
  other arithmetic: 5.38 us -> 0.66 us
    reduce_scatter x1 -> x0, waiting for transfers between devices: 54.2 us -> none  [body(): result = lax.psum_scatter(tile_stack, 'tm', scatter_dimension=2, tiled=True)]
    ppermute x7 -> x16, waiting for transfers between devices: 65.7 us -> 17.6 us  [the longest x8 16.5 us: move(): return lax.ppermute(block, 'chan', route)]
    ppermute x7 -> x16, starting transfers between devices: 8.96 us -> 47.1 us  [the longest x8 37.1 us: move(): return lax.ppermute(block, 'chan', route)]
    pallas_call x0 -> x5, Pallas kernels: none -> 16.7 us  [the longest x4 14.7 us: tiles(): pl.pallas_call(functools.partial(tile_kernel, distances, so_far is None),...]
    unnamed x82 -> x0, local copies, waits for them, and re-layouts: 14.7 us -> none
    dot_general x9 -> x0, matrix products: 11.8 us -> none  [correlate(): jnp.einsum('it,lkt->lik', source, shifted, preferred_element_type=jnp.flo...]
    another operation x9 -> x0, local copies, waits for them, and re-layouts: 10.3 us -> none  [the longest x1 7.89 us: body(): jnp.stack([one_tile(own_block, selected[slot_id], slot_id) for slot_id in...]
    dynamic_update_slice x7 -> x0, local copies, waits for them, and re-layouts: 5.44 us -> none  [body(): _, window = lax.scan(advance, own_block, None, length=REACH)]
  transfers between devices with their start and end apart: 8 -> 16, of which waited for: 8 -> 5; matrix products, arithmetic and copies ran while one was open for 0% -> 2% of each run, Pallas kernels for 0% -> 19%
where the time goes in v1:
time: 84.4 us; the launch traced here: 83.9 us
  starting transfers between devices  47.1 us (56%)
  waiting for transfers between devices  17.6 us (21%)
  Pallas kernels  16.7 us (20%)
  local copies, waits for them, and re-layouts  1.05 us (1%)
  between operations  0.91 us (1%)
    ppermute x8, starting transfers between devices, move(): return lax.ppermute(block, 'chan', route)  37.1 us
    ppermute x8, waiting for transfers between devices, move(): return lax.ppermute(block, 'chan', route)  16.5 us
    pallas_call x4, Pallas kernels, tiles(): pl.pallas_call(functools.partial(tile_kernel, distances, so_far is None),...  14.7 us
    ppermute x8, starting transfers between devices, swap(): return lax.ppermute(block, 'tm', [(0, 1), (1, 0)])  9.94 us
    pallas_call x1, Pallas kernels, stack(): pl.pallas_call(stack_kernel, out_shape=jax.ShapeDtypeStruct((PAIRS * half...  1.97 us
  transfers between devices with their start and end apart: 16, of which 5 were waited for; matrix products, arithmetic and copies ran while one was open for 2% of the time, Pallas kernels for 19%

profile of v1, /device:TPU:1, one launch (start us, length us, event | category | flops | bytes accessed | tf_op | source)
XLA Modules:
  0.0 83.9 jit_solution(2943437197621711421)
XLA Ops:
  0.0 7.7 %collective-permute-start.6 = (bf16[128,1536]{1,0:T(8,128)(2,1)}, bf16[128,1536]{1,0:T(8,128)(2,1)S(1)}, u32[]{:S(2)}, u32[]{:S(2)}) collective-permute-start(bf16[128,1536]{1,0:T(8,128)(2,1)} %bitcast.9), channel_id=1, source_target_pairs={{16,0},{18,2},{20,4},{22,6},{24,8},{26,10},{28,12},{14,14},{32,16}... | collective-permute-start | bytes 1179656 | tf_op jit(solution)/shard_map/ppermute | solution.py:182
  7.7 5.0 %collective-permute-start.1 = (bf16[128,1536]{1,0:T(8,128)(2,1)}, bf16[128,1536]{1,0:T(8,128)(2,1)S(1)}, u32[]{:S(2)}, u32[]{:S(2)}) collective-permute-start(bf16[128,1536]{1,0:T(8,128)(2,1)} %bitcast.10), channel_id=1, source_target_pairs={{2,0},{4,2},{6,4},{8,6},{10,8},{12,10},{14,12},{16,14},{18,16},{20... | collective-permute-start | bytes 1179656 | tf_op jit(solution)/shard_map/ppermute | solution.py:182
  12.7 3.0 %collective-permute-done.6 = bf16[128,1536]{1,0:T(8,128)(2,1)S(1)} collective-permute-done((bf16[128,1536]{1,0:T(8,128)(2,1)}, bf16[128,1536]{1,0:T(8,128)(2,1)S(1)}, u32[]{:S(2)}, u32[]{:S(2)}) %collective-permute-start.6) | collective-permute-done | bytes 393248 | tf_op jit(solution)/shard_map/ppermute | solution.py:182
  15.7 1.6 %collective-permute-start.7 = (bf16[128,1536]{1,0:T(8,128)(2,1)S(1)}, bf16[128,1536]{1,0:T(8,128)(2,1)S(1)}, u32[]{:S(2)}, u32[]{:S(2)}) collective-permute-start(bf16[128,1536]{1,0:T(8,128)(2,1)S(1)} %collective-permute-done.6), channel_id=1, source_target_pairs={{14,0},{0,2},{2,4},{4,6},{6,8},{8,10},{10,12},{12,14},{30,16},{16,... | collective-permute-start | bytes 1179656 | tf_op jit(solution)/shard_map/ppermute | solution.py:182
  17.4 3.4 %collective-permute-done.1.refs_2_ = bf16[128,1536]{1,0:T(8,128)(2,1)S(1)} collective-permute-done((bf16[128,1536]{1,0:T(8,128)(2,1)}, bf16[128,1536]{1,0:T(8,128)(2,1)S(1)}, u32[]{:S(2)}, u32[]{:S(2)}) %collective-permute-start.1) | collective-permute-done | bytes 393248 | tf_op jit(solution)/shard_map/ppermute | solution.py:182
  20.8 7.5 %collective-permute-start.2 = (bf16[128,1536]{1,0:T(8,128)(2,1)S(1)}, bf16[128,1536]{1,0:T(8,128)(2,1)S(1)}, u32[]{:S(2)}, u32[]{:S(2)}) collective-permute-start(bf16[128,1536]{1,0:T(8,128)(2,1)S(1)} %collective-permute-done.1.refs_2_), channel_id=1, source_target_pairs={{2,0},{4,2},{6,4},{8,6},{10,8},{12,10},{14,12},{16,14},{18,16},{20... | collective-permute-start | bytes 1179656 | tf_op jit(solution)/shard_map/ppermute | solution.py:182
  28.3 6.9 %collective-permute-done.2.refs_2_ = bf16[128,1536]{1,0:T(8,128)(2,1)S(1)} collective-permute-done((bf16[128,1536]{1,0:T(8,128)(2,1)S(1)}, bf16[128,1536]{1,0:T(8,128)(2,1)S(1)}, u32[]{:S(2)}, u32[]{:S(2)}) %collective-permute-start.2) | collective-permute-done | bytes 393248 | tf_op jit(solution)/shard_map/ppermute | solution.py:182
  35.2 7.6 %collective-permute-start.3 = (bf16[128,1536]{1,0:T(8,128)(2,1)S(1)}, bf16[128,1536]{1,0:T(8,128)(2,1)S(1)}, u32[]{:S(2)}, u32[]{:S(2)}) collective-permute-start(bf16[128,1536]{1,0:T(8,128)(2,1)S(1)} %collective-permute-done.2.refs_2_), channel_id=1, source_target_pairs={{2,0},{4,2},{6,4},{8,6},{10,8},{12,10},{14,12},{16,14},{18,16},{20... | collective-permute-start | bytes 1179656 | tf_op jit(solution)/shard_map/ppermute | solution.py:182
  42.8 2.7 %collective-permute-start.14 = (bf16[128,1536]{1,0:T(8,128)(2,1)S(1)}, bf16[128,1536]{1,0:T(8,128)(2,1)S(1)}, u32[]{:S(2)}, u32[]{:S(2)}) collective-permute-start(bf16[128,1536]{1,0:T(8,128)(2,1)S(1)} %collective-permute-done.1.refs_2_), channel_id=1, source_target_pairs={{0,1},{1,0},{2,3},{3,2},{4,5},{5,4},{6,7},{7,6},{8,9},{9,8},{10,11... | collective-permute-start | bytes 1179656 | tf_op jit(solution)/shard_map/ppermute | solution.py:185
  45.6 3.2 %collective-permute-done.3.refs_2_ = bf16[128,1536]{1,0:T(8,128)(2,1)S(1)} collective-permute-done((bf16[128,1536]{1,0:T(8,128)(2,1)S(1)}, bf16[128,1536]{1,0:T(8,128)(2,1)S(1)}, u32[]{:S(2)}, u32[]{:S(2)}) %collective-permute-start.3) | collective-permute-done | bytes 393248 | tf_op jit(solution)/shard_map/ppermute | solution.py:182
  48.7 7.6 %collective-permute-start.4 = (bf16[128,1536]{1,0:T(8,128)(2,1)S(1)}, bf16[128,1536]{1,0:T(8,128)(2,1)S(1)}, u32[]{:S(2)}, u32[]{:S(2)}) collective-permute-start(bf16[128,1536]{1,0:T(8,128)(2,1)S(1)} %collective-permute-done.3.refs_2_), channel_id=1, source_target_pairs={{2,0},{4,2},{6,4},{8,6},{10,8},{12,10},{14,12},{16,14},{18,16},{20... | collective-permute-start | bytes 1179656 | tf_op jit(solution)/shard_map/ppermute | solution.py:182
  56.4 1.0 %dynamic-slice_bitcast_fusion = (bf16[64,1536]{1,0:T(8,128)(2,1)S(1)}, bf16[64,1536]{1,0:T(8,128)(2,1)S(1)}) fusion(bf16[1,1,128,1536]{3,2,1,0:T(8,128)(2,1)} %param.3, s32[]{:T(128)S(6)} %select_n.12, s32[]{:T(128)S(6)} %select_n.11), kind=kLoop, calls=%fused_computation | loop fusion | bytes 786440 | tf_op jit(solution)/shard_map/dynamic_slice | solution.py:197
  57.4 3.8 %collective-permute-start = (bf16[64,1536]{1,0:T(8,128)(2,1)S(1)}, bf16[64,1536]{1,0:T(8,128)(2,1)S(1)}, u32[]{:S(2)}, u32[]{:S(2)}) collective-permute-start(bf16[64,1536]{1,0:T(8,128)(2,1)S(1)} %get-tuple-element.5), channel_id=1, source_target_pairs={{0,1},{1,0},{2,3},{3,2},{4,5},{5,4},{6,7},{7,6},{8,9},{9,8},{10,11... | collective-permute-start | bytes 589832 | tf_op jit(solution)/shard_map/ppermute | solution.py:185
  61.2 1.1 %collective-permute-done.second = bf16[64,1536]{1,0:T(8,128)(2,1)S(1)} collective-permute-done((bf16[64,1536]{1,0:T(8,128)(2,1)S(1)}, bf16[64,1536]{1,0:T(8,128)(2,1)S(1)}, u32[]{:S(2)}, u32[]{:S(2)}) %collective-permute-start) | collective-permute-done | bytes 196640 | tf_op jit(solution)/shard_map/ppermute | solution.py:185
  62.3 0.4 collective-permute-start.12
  62.6 0.1 collective-permute-start.13
  62.8 0.4 collective-permute-start.10
  63.3 2.4 %collective-permute-start.5 = (bf16[128,1536]{1,0:T(8,128)(2,1)S(1)}, bf16[128,1536]{1,0:T(8,128)(2,1)S(1)}, u32[]{:S(2)}, u32[]{:S(2)}) collective-permute-start(bf16[128,1536]{1,0:T(8,128)(2,1)S(1)} %collective-permute-done.4.refs_2_), channel_id=1, source_target_pairs={{0,1},{1,0},{2,3},{3,2},{4,5},{5,4},{6,7},{7,6},{8,9},{9,8},{10,11... | collective-permute-start | bytes 1179656 | tf_op jit(solution)/shard_map/ppermute | solution.py:185
  66.4 0.7 compare_select_fusion.refs_0_
  67.0 2.0 %stack.1.refs_1_ = bf16[1088,3200]{1,0:T(8,128)(2,1)S(1)} custom-call(bf16[64,1536]{1,0:T(8,128)(2,1)S(1)} %get-tuple-element.6.first, bf16[64,1536]{1,0:T(8,128)(2,1)S(1)} %collective-permute-done.second), custom_call_target="tpu_custom_call" | custom-call | tf_op jit(solution)/shard_map/stack/pallas_call | solution.py:43
  69.0 7.6 %tiles_1_7.1.refs_6_ = f32[1,3,33,64,128]{4,3,2,1,0:T(8,128)} custom-call(s32[3]{0:T(128)S(1)} %compare_select_fusion.refs_0_, bf16[1088,3200]{1,0:T(8,128)(2,1)S(1)} %stack.1.refs_1_, bf16[128,1536]{1,0:T(8,128)(2,1)S(1)} %collective-permute-done.1.refs_2_, bf16[128,1536]{1,0:T(8,128)(2,1)S(1)} %collective-permute-done.7.refs_3_, ...), custom_call_target="tpu_custom_call" | custom-call | tf_op jit(solution)/shard_map/tiles_1_7/pallas_call | solution.py:148
  76.7 1.3 %tiles_2_6.1.refs_6_ = f32[1,3,33,64,128]{4,3,2,1,0:T(8,128)} custom-call(s32[3]{0:T(128)S(1)} %compare_select_fusion.refs_0_, bf16[1088,3200]{1,0:T(8,128)(2,1)S(1)} %stack.1.refs_1_, bf16[128,1536]{1,0:T(8,128)(2,1)S(1)} %collective-permute-done.2.refs_2_, bf16[128,1536]{1,0:T(8,128)(2,1)} %collective-permute-done.8.refs_3_, ...), custom_call_target="tpu_custom_call", output_to_operand_aliasing={{}: (6, {})} | custom-call | tf_op jit(solution)/shard_map/tiles_2_6/pallas_call | solution.py:148
  78.0 5.1 %tiles_3_5.1.refs_4_ = f32[1,3,33,64,128]{4,3,2,1,0:T(8,128)} custom-call(s32[3]{0:T(128)S(1)} %compare_select_fusion.refs_0_, bf16[1088,3200]{1,0:T(8,128)(2,1)S(1)} %stack.1.refs_1_, bf16[128,1536]{1,0:T(8,128)(2,1)S(1)} %collective-permute-done.3.refs_2_, bf16[128,1536]{1,0:T(8,128)(2,1)} %collective-permute-done.9.refs_3_, ...), custom_call_target="tpu_custom_call", output_to_operand_aliasing={{}: (6, {})} | custom-call | tf_op jit(solution)/shard_map/tiles_3_5/pallas_call | solution.py:148
  83.1 0.6 tiles_4.1
  (15 shorter events, 0.2 us)
Async XLA Ops:
  0.0 15.7 %collective-permute-start.6 = (bf16[128,1536]{1,0:T(8,128)(2,1)}, bf16[128,1536]{1,0:T(8,128)(2,1)S(1)}, u32[]{:S(2)}, u32[]{:S(2)}) collective-permute-start(bf16[128,1536]{1,0:T(8,128)(2,1)} %bitcast.9), channel_id=1, source_target_pairs={{16,0},{18,2},{20,4},{22,6},{24,8},{26,10},{28,12},{14,14},{32,16}... | collective-permute-start | bytes 1179656 | tf_op jit(solution)/shard_map/ppermute | solution.py:182
  7.7 13.1 %collective-permute-start.1 = (bf16[128,1536]{1,0:T(8,128)(2,1)}, bf16[128,1536]{1,0:T(8,128)(2,1)S(1)}, u32[]{:S(2)}, u32[]{:S(2)}) collective-permute-start(bf16[128,1536]{1,0:T(8,128)(2,1)} %bitcast.10), channel_id=1, source_target_pairs={{2,0},{4,2},{6,4},{8,6},{10,8},{12,10},{14,12},{16,14},{18,16},{20... | collective-permute-start | bytes 1179656 | tf_op jit(solution)/shard_map/ppermute | solution.py:182
  15.7 12.6 %collective-permute-start.7 = (bf16[128,1536]{1,0:T(8,128)(2,1)S(1)}, bf16[128,1536]{1,0:T(8,128)(2,1)S(1)}, u32[]{:S(2)}, u32[]{:S(2)}) collective-permute-start(bf16[128,1536]{1,0:T(8,128)(2,1)S(1)} %collective-permute-done.6), channel_id=1, source_target_pairs={{14,0},{0,2},{2,4},{4,6},{6,8},{8,10},{10,12},{12,14},{30,16},{16,... | collective-permute-start | bytes 1179656 | tf_op jit(solution)/shard_map/ppermute | solution.py:182
  20.8 14.4 %collective-permute-start.2 = (bf16[128,1536]{1,0:T(8,128)(2,1)S(1)}, bf16[128,1536]{1,0:T(8,128)(2,1)S(1)}, u32[]{:S(2)}, u32[]{:S(2)}) collective-permute-start(bf16[128,1536]{1,0:T(8,128)(2,1)S(1)} %collective-permute-done.1.refs_2_), channel_id=1, source_target_pairs={{2,0},{4,2},{6,4},{8,6},{10,8},{12,10},{14,12},{16,14},{18,16},{20... | collective-permute-start | bytes 1179656 | tf_op jit(solution)/shard_map/ppermute | solution.py:182
  28.3 17.2 %collective-permute-start.8 = (bf16[128,1536]{1,0:T(8,128)(2,1)S(1)}, bf16[128,1536]{1,0:T(8,128)(2,1)}, u32[]{:S(2)}, u32[]{:S(2)}) collective-permute-start(bf16[128,1536]{1,0:T(8,128)(2,1)S(1)} %collective-permute-done.7.refs_3_), channel_id=1, source_target_pairs={{254,0},{0,2},{2,4},{4,6},{6,8},{8,10},{10,12},{12,14},{14,16},{16... | collective-permute-start | bytes 1179656 | tf_op jit(solution)/shard_map/ppermute | solution.py:182
  35.2 13.6 %collective-permute-start.3 = (bf16[128,1536]{1,0:T(8,128)(2,1)S(1)}, bf16[128,1536]{1,0:T(8,128)(2,1)S(1)}, u32[]{:S(2)}, u32[]{:S(2)}) collective-permute-start(bf16[128,1536]{1,0:T(8,128)(2,1)S(1)} %collective-permute-done.2.refs_2_), channel_id=1, source_target_pairs={{2,0},{4,2},{6,4},{8,6},{10,8},{12,10},{14,12},{16,14},{18,16},{20... | collective-permute-start | bytes 1179656 | tf_op jit(solution)/shard_map/ppermute | solution.py:182
  42.8 19.8 %collective-permute-start.14 = (bf16[128,1536]{1,0:T(8,128)(2,1)S(1)}, bf16[128,1536]{1,0:T(8,128)(2,1)S(1)}, u32[]{:S(2)}, u32[]{:S(2)}) collective-permute-start(bf16[128,1536]{1,0:T(8,128)(2,1)S(1)} %collective-permute-done.1.refs_2_), channel_id=1, source_target_pairs={{0,1},{1,0},{2,3},{3,2},{4,5},{5,4},{6,7},{7,6},{8,9},{9,8},{10,11... | collective-permute-start | bytes 1179656 | tf_op jit(solution)/shard_map/ppermute | solution.py:185
  45.6 17.2 %collective-permute-start.15 = (bf16[128,1536]{1,0:T(8,128)(2,1)S(1)}, bf16[128,1536]{1,0:T(8,128)(2,1)S(1)}, u32[]{:S(2)}, u32[]{:S(2)}) collective-permute-start(bf16[128,1536]{1,0:T(8,128)(2,1)S(1)} %collective-permute-done.7.refs_3_), channel_id=1, source_target_pairs={{0,1},{1,0},{2,3},{3,2},{4,5},{5,4},{6,7},{7,6},{8,9},{9,8},{10,11... | collective-permute-start | bytes 1179656 | tf_op jit(solution)/shard_map/ppermute | solution.py:185
  45.6 17.6 %collective-permute-start.9 = (bf16[128,1536]{1,0:T(8,128)(2,1)}, bf16[128,1536]{1,0:T(8,128)(2,1)}, u32[]{:S(2)}, u32[]{:S(2)}) collective-permute-start(bf16[128,1536]{1,0:T(8,128)(2,1)} %collective-permute-done.8.refs_3_), channel_id=1, source_target_pairs={{254,0},{0,2},{2,4},{4,6},{6,8},{8,10},{10,12},{12,14},{14,16},{16... | collective-permute-start | bytes 1179656 | tf_op jit(solution)/shard_map/ppermute | solution.py:182
  48.7 14.5 %collective-permute-start.4 = (bf16[128,1536]{1,0:T(8,128)(2,1)S(1)}, bf16[128,1536]{1,0:T(8,128)(2,1)S(1)}, u32[]{:S(2)}, u32[]{:S(2)}) collective-permute-start(bf16[128,1536]{1,0:T(8,128)(2,1)S(1)} %collective-permute-done.3.refs_2_), channel_id=1, source_target_pairs={{2,0},{4,2},{6,4},{8,6},{10,8},{12,10},{14,12},{16,14},{18,16},{20... | collective-permute-start | bytes 1179656 | tf_op jit(solution)/shard_map/ppermute | solution.py:182
  57.4 4.8 %collective-permute-start = (bf16[64,1536]{1,0:T(8,128)(2,1)S(1)}, bf16[64,1536]{1,0:T(8,128)(2,1)S(1)}, u32[]{:S(2)}, u32[]{:S(2)}) collective-permute-start(bf16[64,1536]{1,0:T(8,128)(2,1)S(1)} %get-tuple-element.5), channel_id=1, source_target_pairs={{0,1},{1,0},{2,3},{3,2},{4,5},{5,4},{6,7},{7,6},{8,9},{9,8},{10,11... | collective-permute-start | bytes 589832 | tf_op jit(solution)/shard_map/ppermute | solution.py:185
  62.3 14.4 %collective-permute-start.12 = (bf16[128,1536]{1,0:T(8,128)(2,1)S(1)}, bf16[128,1536]{1,0:T(8,128)(2,1)}, u32[]{:S(2)}, u32[]{:S(2)}) collective-permute-start(bf16[128,1536]{1,0:T(8,128)(2,1)S(1)} %collective-permute-done.2.refs_2_), channel_id=1, source_target_pairs={{0,1},{1,0},{2,3},{3,2},{4,5},{5,4},{6,7},{7,6},{8,9},{9,8},{10,11... | collective-permute-start | bytes 1179656 | tf_op jit(solution)/shard_map/ppermute | solution.py:185
  62.6 14.0 %collective-permute-start.13 = (bf16[128,1536]{1,0:T(8,128)(2,1)}, bf16[128,1536]{1,0:T(8,128)(2,1)}, u32[]{:S(2)}, u32[]{:S(2)}) collective-permute-start(bf16[128,1536]{1,0:T(8,128)(2,1)} %collective-permute-done.8.refs_3_), channel_id=1, source_target_pairs={{0,1},{1,0},{2,3},{3,2},{4,5},{5,4},{6,7},{7,6},{8,9},{9,8},{10,11... | collective-permute-start | bytes 1179656 | tf_op jit(solution)/shard_map/ppermute | solution.py:185
  62.8 15.2 %collective-permute-start.10 = (bf16[128,1536]{1,0:T(8,128)(2,1)S(1)}, bf16[128,1536]{1,0:T(8,128)(2,1)}, u32[]{:S(2)}, u32[]{:S(2)}) collective-permute-start(bf16[128,1536]{1,0:T(8,128)(2,1)S(1)} %collective-permute-done.3.refs_2_), channel_id=1, source_target_pairs={{0,1},{1,0},{2,3},{3,2},{4,5},{5,4},{6,7},{7,6},{8,9},{9,8},{10,11... | collective-permute-start | bytes 1179656 | tf_op jit(solution)/shard_map/ppermute | solution.py:185
  63.2 14.9 %collective-permute-start.11 = (bf16[128,1536]{1,0:T(8,128)(2,1)}, bf16[128,1536]{1,0:T(8,128)(2,1)}, u32[]{:S(2)}, u32[]{:S(2)}) collective-permute-start(bf16[128,1536]{1,0:T(8,128)(2,1)} %collective-permute-done.9.refs_3_), channel_id=1, source_target_pairs={{0,1},{1,0},{2,3},{3,2},{4,5},{5,4},{6,7},{7,6},{8,9},{9,8},{10,11... | collective-permute-start | bytes 1179656 | tf_op jit(solution)/shard_map/ppermute | solution.py:185
  63.3 19.8 %collective-permute-start.5 = (bf16[128,1536]{1,0:T(8,128)(2,1)S(1)}, bf16[128,1536]{1,0:T(8,128)(2,1)S(1)}, u32[]{:S(2)}, u32[]{:S(2)}) collective-permute-start(bf16[128,1536]{1,0:T(8,128)(2,1)S(1)} %collective-permute-done.4.refs_2_), channel_id=1, source_target_pairs={{0,1},{1,0},{2,3},{3,2},{4,5},{5,4},{6,7},{7,6},{8,9},{9,8},{10,11... | collective-permute-start | bytes 1179656 | tf_op jit(solution)/shard_map/ppermute | solution.py:185

commit v2 on v0

v2 whole, which is shorter than its diff:
```python
import functools

import jax
import jax.numpy as jnp
from jax import lax
from jax.experimental import pallas as pl
from jax.experimental.pallas import tpu as pltpu
from jax.sharding import PartitionSpec as P

MAXLAG = 16
REACH = 7
P_MAX = 3
LAGS = 2 * MAXLAG + 1
PAIRS = MAXLAG + 1
EDGE = 128
FREE = pl.CostEstimate(flops=0, bytes_accessed=0, transcendentals=0)
VMEM = pl.BlockSpec(memory_space=pltpu.VMEM)
SMEM = pl.BlockSpec(memory_space=pltpu.SMEM)
ANY = pl.BlockSpec(memory_space=pl.ANY)


def stack_kernel(wanted, first, second, out, result, padded, empty, sem):
    half, samples = first.shape
    empty[...] = jnp.zeros_like(empty)
    for action in ("start", "wait"):
        for slot in range(P_MAX):

            @pl.when(wanted[slot] == 0)
            def _(slot=slot):
                copy = pltpu.make_async_copy(empty, result.at[0, slot], sem)
                copy.start() if action == "start" else copy.wait()

        if action == "wait":
            return
        padded[...] = jnp.zeros_like(padded)
        for g, source in enumerate((first, second)):
            padded[:, EDGE : EDGE + samples] = source[...]
            for m in range(PAIRS):
                start = EDGE + MAXLAG - 2 * m
                out[m * half : (m + 1) * half, g * samples : (g + 1) * samples] = padded[:, start : start + samples]
        lane = lax.broadcasted_iota(jnp.int32, (half, EDGE), 1)
        for m in range(PAIRS):
            at = MAXLAG - 1 - 2 * m
            edge = jnp.zeros((half, EDGE), jnp.float32)
            if at >= 0:
                for g, source in enumerate((first, second)):
                    column = source[:, :EDGE].astype(jnp.float32)[:, at : at + 1]
                    edge = jnp.where(lane == g, column, edge)
            out[m * half : (m + 1) * half, 2 * samples :] = edge.astype(jnp.bfloat16)


def stack(wanted, first, second):
    half, samples = first.shape
    return pl.pallas_call(
        stack_kernel,
        out_shape=[
            pltpu.VMEM((PAIRS * half, 2 * samples + EDGE), jnp.bfloat16),
            jax.ShapeDtypeStruct((1, P_MAX, LAGS, half, 2 * half), jnp.float32),
        ],
        in_specs=[SMEM, VMEM, VMEM],
        out_specs=[VMEM, ANY],
        scratch_shapes=[
            pltpu.VMEM((half, samples + 2 * EDGE), jnp.bfloat16),
            pltpu.VMEM((LAGS, half, 2 * half), jnp.float32),
            pltpu.SemaphoreType.DMA,
        ],
        compiler_params=pltpu.CompilerParams(vmem_limit_bytes=24 * 2**20),
        cost_estimate=FREE,
        name="stack",
    )(wanted, first, second)


def fill_columns(own, other, columns):
    count = columns.shape[0] // 2
    at = 0
    for pair in zip(own, other):
        size, samples = pair[0].shape
        low, high = pl.ds(at, size), pl.ds(count + at, size)
        lane = lax.broadcasted_iota(jnp.int32, (size, EDGE), 1)
        edge = jnp.zeros((size, EDGE), jnp.float32)
        for g, target in enumerate(pair):
            block = target[...]
            columns[low, g * samples : (g + 1) * samples] = block
            ahead = jnp.concatenate([block[:, 1:], jnp.zeros((size, 1), block.dtype)], 1)
            columns[high, g * samples : (g + 1) * samples] = ahead
            edge = jnp.where(lane == g, block[:, :EDGE].astype(jnp.float32)[:, :1], edge)
        columns[low, 2 * samples :] = jnp.zeros((size, EDGE), jnp.bfloat16)
        columns[high, 2 * samples :] = edge.astype(jnp.bfloat16)
        at += size


def is_in(distance, distances):
    found = distance == distances[0]
    for d in distances[1:]:
        found = jnp.logical_or(found, distance == d)
    return found


def pick_kernel(distances, counts, wanted, *refs):
    n = sum(counts)
    parts, outs, sem = list(refs[:n]), refs[n:-1], refs[-1]
    blocks = [[parts.pop(0) for _ in range(c)] for c in counts]

    for action in ("start", "wait"):
        for slot in range(P_MAX):
            for d, block in zip(distances, blocks):

                @pl.when(wanted[slot] == d)
                def _(slot=slot, block=block):
                    size = block[0].shape[0]
                    for h, part in enumerate(block):
                        copy = pltpu.make_async_copy(part, outs[slot].at[pl.ds(h * size, size)], sem)
                        copy.start() if action == "start" else copy.wait()


def pick(distances, wanted, blocks):
    counts = [len(block) for block in blocks]
    size, samples = blocks[0][0].shape
    shape = jax.ShapeDtypeStruct((size * counts[0], samples), jnp.bfloat16)
    parts = [part for block in blocks for part in block]
    picked = pl.pallas_call(
        functools.partial(pick_kernel, distances, counts),
        out_shape=[shape] * P_MAX,
        in_specs=[SMEM] + [ANY] * len(parts),
        out_specs=[ANY] * P_MAX,
        scratch_shapes=[pltpu.SemaphoreType.DMA],
        compiler_params=pltpu.CompilerParams(vmem_limit_bytes=8 * 2**20),
        cost_estimate=FREE,
        name="pick",
    )(wanted, *parts)
    return list(picked)


def tile_kernel(distances, wanted, rows, *refs):
    own, other = refs[:P_MAX], refs[P_MAX : 2 * P_MAX]
    out, columns, tile, sem = refs[-4:]
    count = columns.shape[0] // 2
    half = rows.shape[0] // PAIRS

    @pl.loop(0, P_MAX)
    def _(slot):
        @pl.when(is_in(wanted[slot], distances))
        def _():
            for k in range(P_MAX):

                @pl.when(slot == k)
                def _(k=k):
                    fill_columns(own[k : k + 1], other[k : k + 1], columns)

            got = lax.dot_general(
                rows[...], columns[...], (((1,), (1,)), ((), ())), preferred_element_type=jnp.float32
            )
            for m in range(PAIRS):
                part = got[m * half : (m + 1) * half]
                tile[2 * m] = part[:, :count]
                if 2 * m + 1 < LAGS:
                    tile[2 * m + 1] = part[:, count:]
            copy = pltpu.make_async_copy(tile, out.at[0, slot], sem)
            copy.start()
            copy.wait()


def tiles(distances, wanted, stacked, own, other, so_far):
    rows = stacked.shape
    half = rows[0] // PAIRS
    count = 2 * half
    stacked = pltpu.with_memory_space_constraint(stacked, pltpu.VMEM)
    arguments = [wanted, stacked, *own, *other, so_far]
    return pl.pallas_call(
        functools.partial(tile_kernel, distances),
        out_shape=jax.ShapeDtypeStruct(so_far.shape, so_far.dtype),
        in_specs=[SMEM] + [VMEM] * (len(arguments) - 2) + [ANY],
        out_specs=ANY,
        scratch_shapes=[
            pltpu.VMEM((2 * count, rows[1]), jnp.bfloat16),
            pltpu.VMEM((LAGS, half, count), jnp.float32),
            pltpu.SemaphoreType.DMA,
        ],
        input_output_aliases={len(arguments) - 1: 0},
        compiler_params=pltpu.CompilerParams(vmem_limit_bytes=16 * 2**20),
        cost_estimate=FREE,
        name="tiles_" + "_".join(map(str, distances)),
    )(*arguments)


def body(traces, pair_target, pair_count):
    own = traces[0, 0]
    half = own.shape[0] // 2
    blocks = lax.axis_size("chan")
    me, core = lax.axis_index("chan"), lax.axis_index("tm")
    slots = jnp.arange(P_MAX, dtype=jnp.int32)
    wanted = jnp.where(slots < pair_count[0], pair_target[0] - me, 0).astype(jnp.int32)

    row = 8
    everyone = range(blocks)
    down = [((i + 1) % blocks, i) for i in everyone]
    up = [((i - 1) % blocks, i) for i in everyone]
    next_row = [((i + row) % blocks, i) if i % row < row - 1 else (i, i) for i in everyone]
    turn = [(i - 1, i) if i % row else (i + row - 1, i) for i in everyone]

    def move(parts, route):
        return [lax.ppermute(p, "chan", route) for p in parts]

    def swap(parts):
        return [lax.ppermute(p, "tm", [(0, 1), (1, 0)]) for p in parts]

    def step(*values):
        return lax.optimization_barrier(values)

    mine = lax.dynamic_slice_in_dim(own, core * half, half, 0)
    theirs = lax.dynamic_slice_in_dim(own, (1 - core) * half, half, 0)
    d1 = move([own], down)
    below = move([own], next_row)
    theirs = swap([theirs])[0]
    rows, result = stack(wanted, mine, theirs)
    below, rows, result = step(below, rows, result)
    d7 = move(below, turn)
    d2 = move(d1, down)
    d6 = move(d7, up)
    d3 = move(d2, down)
    d5 = move(d6, up)
    d4 = move(d3, down)
    near = pick((1, 7, 2, 6), wanted, [d1, d7, d2, d6])
    result = tiles((1, 7, 2, 6), wanted, rows, near, swap(near), result)
    d3, d5, d4, result = step(d3, d5, d4, result)
    far = pick((3, 5, 4), wanted, [d3, d5, d4])
    return tiles((3, 5, 4), wanted, rows, far, swap(far), result)


def solution(mesh):
    placed = (P("tm", "chan", None, None), P("chan", None), P("chan"))
    return jax.shard_map(
        body,
        mesh=mesh,
        in_specs=placed,
        out_specs=P("chan", None, None, "tm", None),
        check_vma=False,
    )
```

time: 199 us -> 75 us (0.38)
  waiting for transfers between devices: 120 us -> 15.3 us
  local copies, waits for them, and re-layouts: 37.5 us -> 1.05 us
  starting transfers between devices: 8.96 us -> 41.3 us
  Pallas kernels: 0 us -> 15.7 us
  between operations: 14.5 us -> 0.89 us
  matrix products: 11.8 us -> 0 us
  other arithmetic: 5.38 us -> 0.66 us
    reduce_scatter x1 -> x0, waiting for transfers between devices: 54.2 us -> none  [body(): result = lax.psum_scatter(tile_stack, 'tm', scatter_dimension=2, tiled=True)]
    ppermute x7 -> x15, waiting for transfers between devices: 65.7 us -> 15.3 us  [the longest x8 13.3 us: move(): return [lax.ppermute(p, 'chan', route) for p in parts]]
    ppermute x7 -> x15, starting transfers between devices: 8.96 us -> 41.3 us  [the longest x8 35.1 us: move(): return [lax.ppermute(p, 'chan', route) for p in parts]]
    pallas_call x0 -> x5, Pallas kernels: none -> 15.7 us  [the longest x2 11.2 us: tiles(): pl.pallas_call(functools.partial(tile_kernel, distances), out_shape=jax.S...]
    unnamed x82 -> x0, local copies, waits for them, and re-layouts: 14.7 us -> none
    dot_general x9 -> x0, matrix products: 11.8 us -> none  [correlate(): jnp.einsum('it,lkt->lik', source, shifted, preferred_element_type=jnp.flo...]
    another operation x9 -> x0, local copies, waits for them, and re-layouts: 10.3 us -> none  [the longest x1 7.89 us: body(): jnp.stack([one_tile(own_block, selected[slot_id], slot_id) for slot_id in...]
    dynamic_update_slice x7 -> x0, local copies, waits for them, and re-layouts: 5.44 us -> none  [body(): _, window = lax.scan(advance, own_block, None, length=REACH)]
  transfers between devices with their start and end apart: 8 -> 15, of which waited for: 8 -> 8; matrix products, arithmetic and copies ran while one was open for 0% -> 2% of each run, Pallas kernels for 0% -> 15%
where the time goes in v2:
time: 75 us; the launch traced here: 74.9 us
  starting transfers between devices  41.3 us (55%)
  Pallas kernels  15.7 us (21%)
  waiting for transfers between devices  15.3 us (20%)
  local copies, waits for them, and re-layouts  1.05 us (1%)
  between operations  0.89 us (1%)
    ppermute x8, starting transfers between devices, move(): return [lax.ppermute(p, 'chan', route) for p in parts]  35.1 us
    ppermute x8, waiting for transfers between devices, move(): return [lax.ppermute(p, 'chan', route) for p in parts]  13.3 us
    pallas_call x2, Pallas kernels, tiles(): pl.pallas_call(functools.partial(tile_kernel, distances), out_shape=jax.S...  11.2 us
    ppermute x7, starting transfers between devices, swap(): return [lax.ppermute(p, 'tm', [(0, 1), (1, 0)]) for p in parts]  6.17 us
    pallas_call x1, Pallas kernels, stack(): pl.pallas_call(stack_kernel, out_shape=[pltpu.VMEM((PAIRS * half, 2 * sam...  2.56 us
    ppermute x7, waiting for transfers between devices, swap(): return [lax.ppermute(p, 'tm', [(0, 1), (1, 0)]) for p in parts]  1.97 us
    pallas_call x2, Pallas kernels, pick(): pl.pallas_call(functools.partial(pick_kernel, distances, counts), out_sha...  1.92 us
  transfers between devices with their start and end apart: 15, of which 8 were waited for; matrix products, arithmetic and copies ran while one was open for 2% of the time, Pallas kernels for 15%

profile of v2, /device:TPU:1, one launch (start us, length us, event | category | flops | bytes accessed | tf_op | source)
XLA Modules:
  0.0 74.9 jit_solution(14713972447319657315)
XLA Ops:
  0.0 7.7 %collective-permute-start = (bf16[128,1536]{1,0:T(8,128)(2,1)}, bf16[128,1536]{1,0:T(8,128)(2,1)S(1)}, u32[]{:S(2)}, u32[]{:S(2)}) collective-permute-start(bf16[128,1536]{1,0:T(8,128)(2,1)} %bitcast.9), channel_id=1, source_target_pairs={{16,0},{18,2},{20,4},{22,6},{24,8},{26,10},{28,12},{14,14},{32,16}... | collective-permute-start | bytes 1179656 | tf_op jit(solution)/shard_map/ppermute | solution.py:202
  7.7 5.0 %collective-permute-start.2 = (bf16[128,1536]{1,0:T(8,128)(2,1)}, bf16[128,1536]{1,0:T(8,128)(2,1)S(1)}, u32[]{:S(2)}, u32[]{:S(2)}) collective-permute-start(bf16[128,1536]{1,0:T(8,128)(2,1)} %bitcast.10), channel_id=1, source_target_pairs={{2,0},{4,2},{6,4},{8,6},{10,8},{12,10},{14,12},{16,14},{18,16},{20... | collective-permute-start | bytes 1179656 | tf_op jit(solution)/shard_map/ppermute | solution.py:202
  12.7 1.0 %dynamic-slice_bitcast_fusion = (bf16[64,1536]{1,0:T(8,128)(2,1)S(1)}, bf16[64,1536]{1,0:T(8,128)(2,1)S(1)}) fusion(bf16[1,1,128,1536]{3,2,1,0:T(8,128)(2,1)} %param.3, s32[]{:T(128)S(6)} %select_n.12, s32[]{:T(128)S(6)} %select_n.11), kind=kLoop, calls=%fused_computation | loop fusion | bytes 786440 | tf_op jit(solution)/shard_map/dynamic_slice | solution.py:211
  13.7 1.0 %collective-permute-start.1 = (bf16[64,1536]{1,0:T(8,128)(2,1)S(1)}, bf16[64,1536]{1,0:T(8,128)(2,1)S(1)}, u32[]{:S(2)}, u32[]{:S(2)}) collective-permute-start(bf16[64,1536]{1,0:T(8,128)(2,1)S(1)} %get-tuple-element.35), channel_id=1, source_target_pairs={{0,1},{1,0},{2,3},{3,2},{4,5},{5,4},{6,7},{7,6},{8,9},{9,8},{10,11... | collective-permute-start | bytes 589832 | tf_op jit(solution)/shard_map/ppermute | solution.py:205
  15.4 0.7 compare_select_fusion.wanted
  16.1 2.6 %stack.1 = (bf16[1088,3200]{1,0:T(8,128)(2,1)S(1)}, f32[1,3,33,64,128]{4,3,2,1,0:T(8,128)}) custom-call(s32[3]{0:T(128)S(1)} %compare_select_fusion.wanted, bf16[64,1536]{1,0:T(8,128)(2,1)S(1)} %get-tuple-element.36.first, bf16[64,1536]{1,0:T(8,128)(2,1)S(1)} %collective-permute-done.1.second), custom_call_target="tpu_custom_call" | custom-call | tf_op jit(solution)/shard_map/stack/pallas_call | solution.py:54
  18.8 2.0 %collective-permute-done.2.refs_0_ = bf16[128,1536]{1,0:T(8,128)(2,1)S(1)} collective-permute-done((bf16[128,1536]{1,0:T(8,128)(2,1)}, bf16[128,1536]{1,0:T(8,128)(2,1)S(1)}, u32[]{:S(2)}, u32[]{:S(2)}) %collective-permute-start.2) | collective-permute-done | bytes 393248 | tf_op jit(solution)/shard_map/ppermute | solution.py:202
  20.8 7.5 %collective-permute-start.3 = (bf16[128,1536]{1,0:T(8,128)(2,1)S(1)}, bf16[128,1536]{1,0:T(8,128)(2,1)S(1)}, u32[]{:S(2)}, u32[]{:S(2)}) collective-permute-start(bf16[128,1536]{1,0:T(8,128)(2,1)S(1)} %collective-permute-done.2.refs_0_), channel_id=1, source_target_pairs={{2,0},{4,2},{6,4},{8,6},{10,8},{12,10},{14,12},{16,14},{18,16},{20... | collective-permute-start | bytes 1179656 | tf_op jit(solution)/shard_map/ppermute | solution.py:202
  28.3 2.2 %collective-permute-done.5.refs_1_ = bf16[128,1536]{1,0:T(8,128)(2,1)S(1)} collective-permute-done((bf16[128,1536]{1,0:T(8,128)(2,1)S(1)}, bf16[128,1536]{1,0:T(8,128)(2,1)S(1)}, u32[]{:S(2)}, u32[]{:S(2)}) %collective-permute-start.5) | collective-permute-done | bytes 393248 | tf_op jit(solution)/shard_map/ppermute | solution.py:202
  30.6 4.6 %collective-permute-done.3.refs_2_ = bf16[128,1536]{1,0:T(8,128)(2,1)S(1)} collective-permute-done((bf16[128,1536]{1,0:T(8,128)(2,1)S(1)}, bf16[128,1536]{1,0:T(8,128)(2,1)S(1)}, u32[]{:S(2)}, u32[]{:S(2)}) %collective-permute-start.3) | collective-permute-done | bytes 393248 | tf_op jit(solution)/shard_map/ppermute | solution.py:202
  35.2 7.6 %collective-permute-start.4 = (bf16[128,1536]{1,0:T(8,128)(2,1)S(1)}, bf16[128,1536]{1,0:T(8,128)(2,1)S(1)}, u32[]{:S(2)}, u32[]{:S(2)}) collective-permute-start(bf16[128,1536]{1,0:T(8,128)(2,1)S(1)} %collective-permute-done.3.refs_2_), channel_id=1, source_target_pairs={{2,0},{4,2},{6,4},{8,6},{10,8},{12,10},{14,12},{16,14},{18,16},{20... | collective-permute-start | bytes 1179656 | tf_op jit(solution)/shard_map/ppermute | solution.py:202
  42.8 2.8 %collective-permute-done.6.refs_3_ = bf16[128,1536]{1,0:T(8,128)(2,1)S(1)} collective-permute-done((bf16[128,1536]{1,0:T(8,128)(2,1)S(1)}, bf16[128,1536]{1,0:T(8,128)(2,1)S(1)}, u32[]{:S(2)}, u32[]{:S(2)}) %collective-permute-start.6) | collective-permute-done | bytes 393248 | tf_op jit(solution)/shard_map/ppermute | solution.py:202
  45.7 1.1 %pick.2 = (bf16[128,1536]{1,0:T(8,128)(2,1)S(1)}, bf16[128,1536]{1,0:T(8,128)(2,1)S(1)}, bf16[128,1536]{1,0:T(8,128)(2,1)S(1)}) custom-call(s32[3]{0:T(128)S(1)} %compare_select_fusion.wanted, bf16[128,1536]{1,0:T(8,128)(2,1)S(1)} %collective-permute-done.2.refs_0_, bf16[128,1536]{1,0:T(8,128)(2,1)S(1)} %collective-permute-done.5.refs_1_, ...), custom_call_target="tpu_custom_call" | custom-call | tf_op jit(solution)/shard_map/pick/pallas_call | solution.py:121
  46.7 1.9 %collective-permute-start.10 = (bf16[128,1536]{1,0:T(8,128)(2,1)S(1)}, bf16[128,1536]{1,0:T(8,128)(2,1)S(1)}, u32[]{:S(2)}, u32[]{:S(2)}) collective-permute-start(bf16[128,1536]{1,0:T(8,128)(2,1)S(1)} %get-tuple-element.25.refs_1_), channel_id=1, source_target_pairs={{0,1},{1,0},{2,3},{3,2},{4,5},{5,4},{6,7},{7,6},{8,9},{9,8},{10,11... | collective-permute-start | bytes 1179656 | tf_op jit(solution)/shard_map/ppermute | solution.py:205
  48.8 0.4 collective-permute-start.9
  49.2 7.2 %collective-permute-start.8 = (bf16[128,1536]{1,0:T(8,128)(2,1)S(1)}, bf16[128,1536]{1,0:T(8,128)(2,1)S(1)}, u32[]{:S(2)}, u32[]{:S(2)}) collective-permute-start(bf16[128,1536]{1,0:T(8,128)(2,1)S(1)} %collective-permute-done.4.refs_0_), channel_id=1, source_target_pairs={{2,0},{4,2},{6,4},{8,6},{10,8},{12,10},{14,12},{16,14},{18,16},{20... | collective-permute-start | bytes 1179656 | tf_op jit(solution)/shard_map/ppermute | solution.py:202
  56.4 7.3 %tiles_1_7_2_6.1.refs_6_ = f32[1,3,33,64,128]{4,3,2,1,0:T(8,128)} custom-call(s32[3]{0:T(128)S(1)} %compare_select_fusion.wanted, bf16[1088,3200]{1,0:T(8,128)(2,1)S(1)} %get-tuple-element.22.rows, bf16[128,1536]{1,0:T(8,128)(2,1)S(1)} %get-tuple-element.24.refs_0_, bf16[128,1536]{1,0:T(8,128)(2,1)S(1)} %get-tuple-element.25.refs_1_, ...), custom_call_target="tpu_custom_call", output_to_operand_aliasing={{}: (8, {})} | custom-call | tf_op jit(solution)/shard_map/tiles_1_7_2_6/pallas_call | solution.py:169
  63.7 1.6 %collective-permute-done.7.refs_1_ = bf16[128,1536]{1,0:T(8,128)(2,1)S(1)} collective-permute-done((bf16[128,1536]{1,0:T(8,128)(2,1)S(1)}, bf16[128,1536]{1,0:T(8,128)(2,1)S(1)}, u32[]{:S(2)}, u32[]{:S(2)}) %collective-permute-start.7) | collective-permute-done | bytes 393248 | tf_op jit(solution)/shard_map/ppermute | solution.py:202
  65.3 0.8 %pick.3 = (bf16[128,1536]{1,0:T(8,128)(2,1)S(1)}, bf16[128,1536]{1,0:T(8,128)(2,1)S(1)}, bf16[128,1536]{1,0:T(8,128)(2,1)S(1)}) custom-call(s32[3]{0:T(128)S(1)} %compare_select_fusion.wanted, bf16[128,1536]{1,0:T(8,128)(2,1)S(1)} %collective-permute-done.4.refs_0_, bf16[128,1536]{1,0:T(8,128)(2,1)S(1)} %collective-permute-done.7.refs_1_, ...), custom_call_target="tpu_custom_call" | custom-call | tf_op jit(solution)/shard_map/pick/pallas_call | solution.py:121
  66.2 2.2 %collective-permute-start.12 = (bf16[128,1536]{1,0:T(8,128)(2,1)S(1)}, bf16[128,1536]{1,0:T(8,128)(2,1)S(1)}, u32[]{:S(2)}, u32[]{:S(2)}) collective-permute-start(bf16[128,1536]{1,0:T(8,128)(2,1)S(1)} %get-tuple-element.31.refs_0_), channel_id=1, source_target_pairs={{0,1},{1,0},{2,3},{3,2},{4,5},{5,4},{6,7},{7,6},{8,9},{9,8},{10,11... | collective-permute-start | bytes 1179656 | tf_op jit(solution)/shard_map/ppermute | solution.py:205
  68.8 0.8 %collective-permute-done.12.refs_3_ = bf16[128,1536]{1,0:T(8,128)(2,1)S(1)} collective-permute-done((bf16[128,1536]{1,0:T(8,128)(2,1)S(1)}, bf16[128,1536]{1,0:T(8,128)(2,1)S(1)}, u32[]{:S(2)}, u32[]{:S(2)}) %collective-permute-start.12) | collective-permute-done | bytes 393248 | tf_op jit(solution)/shard_map/ppermute | solution.py:205
  69.7 0.6 collective-permute-done.13.refs_4_
  70.2 0.6 collective-permute-done.14.refs_5_
  70.8 4.0 %tiles_3_5_4.1 = f32[1,3,33,64,128]{4,3,2,1,0:T(8,128)} custom-call(s32[3]{0:T(128)S(1)} %compare_select_fusion.wanted, bf16[1088,3200]{1,0:T(8,128)(2,1)S(1)} %get-tuple-element.22.rows, bf16[128,1536]{1,0:T(8,128)(2,1)S(1)} %get-tuple-element.31.refs_0_, bf16[128,1536]{1,0:T(8,128)(2,1)S(1)} %get-tuple-element.32.refs_1_, ...), custom_call_target="tpu_custom_call", output_to_operand_aliasing={{}: (8, {})} | custom-call | tf_op jit(solution)/shard_map/tiles_3_5_4/pallas_call | solution.py:169
  (13 shorter events, 0.7 us)
Async XLA Ops:
  0.0 18.7 %collective-permute-start = (bf16[128,1536]{1,0:T(8,128)(2,1)}, bf16[128,1536]{1,0:T(8,128)(2,1)S(1)}, u32[]{:S(2)}, u32[]{:S(2)}) collective-permute-start(bf16[128,1536]{1,0:T(8,128)(2,1)} %bitcast.9), channel_id=1, source_target_pairs={{16,0},{18,2},{20,4},{22,6},{24,8},{26,10},{28,12},{14,14},{32,16}... | collective-permute-start | bytes 1179656 | tf_op jit(solution)/shard_map/ppermute | solution.py:202
  7.7 13.1 %collective-permute-start.2 = (bf16[128,1536]{1,0:T(8,128)(2,1)}, bf16[128,1536]{1,0:T(8,128)(2,1)S(1)}, u32[]{:S(2)}, u32[]{:S(2)}) collective-permute-start(bf16[128,1536]{1,0:T(8,128)(2,1)} %bitcast.10), channel_id=1, source_target_pairs={{2,0},{4,2},{6,4},{8,6},{10,8},{12,10},{14,12},{16,14},{18,16},{20... | collective-permute-start | bytes 1179656 | tf_op jit(solution)/shard_map/ppermute | solution.py:202
  13.7 2.4 %collective-permute-start.1 = (bf16[64,1536]{1,0:T(8,128)(2,1)S(1)}, bf16[64,1536]{1,0:T(8,128)(2,1)S(1)}, u32[]{:S(2)}, u32[]{:S(2)}) collective-permute-start(bf16[64,1536]{1,0:T(8,128)(2,1)S(1)} %get-tuple-element.35), channel_id=1, source_target_pairs={{0,1},{1,0},{2,3},{3,2},{4,5},{5,4},{6,7},{7,6},{8,9},{9,8},{10,11... | collective-permute-start | bytes 589832 | tf_op jit(solution)/shard_map/ppermute | solution.py:205
  18.7 11.9 %collective-permute-start.5 = (bf16[128,1536]{1,0:T(8,128)(2,1)S(1)}, bf16[128,1536]{1,0:T(8,128)(2,1)S(1)}, u32[]{:S(2)}, u32[]{:S(2)}) collective-permute-start(bf16[128,1536]{1,0:T(8,128)(2,1)S(1)} %collective-permute-done), channel_id=1, source_target_pairs={{14,0},{0,2},{2,4},{4,6},{6,8},{8,10},{10,12},{12,14},{30,16},{16,... | collective-permute-start | bytes 1179656 | tf_op jit(solution)/shard_map/ppermute | solution.py:202
  20.8 14.4 %collective-permute-start.3 = (bf16[128,1536]{1,0:T(8,128)(2,1)S(1)}, bf16[128,1536]{1,0:T(8,128)(2,1)S(1)}, u32[]{:S(2)}, u32[]{:S(2)}) collective-permute-start(bf16[128,1536]{1,0:T(8,128)(2,1)S(1)} %collective-permute-done.2.refs_0_), channel_id=1, source_target_pairs={{2,0},{4,2},{6,4},{8,6},{10,8},{12,10},{14,12},{16,14},{18,16},{20... | collective-permute-start | bytes 1179656 | tf_op jit(solution)/shard_map/ppermute | solution.py:202
  30.6 15.1 %collective-permute-start.6 = (bf16[128,1536]{1,0:T(8,128)(2,1)S(1)}, bf16[128,1536]{1,0:T(8,128)(2,1)S(1)}, u32[]{:S(2)}, u32[]{:S(2)}) collective-permute-start(bf16[128,1536]{1,0:T(8,128)(2,1)S(1)} %collective-permute-done.5.refs_1_), channel_id=1, source_target_pairs={{254,0},{0,2},{2,4},{4,6},{6,8},{8,10},{10,12},{12,14},{14,16},{16... | collective-permute-start | bytes 1179656 | tf_op jit(solution)/shard_map/ppermute | solution.py:202
  35.2 14.0 %collective-permute-start.4 = (bf16[128,1536]{1,0:T(8,128)(2,1)S(1)}, bf16[128,1536]{1,0:T(8,128)(2,1)S(1)}, u32[]{:S(2)}, u32[]{:S(2)}) collective-permute-start(bf16[128,1536]{1,0:T(8,128)(2,1)S(1)} %collective-permute-done.3.refs_2_), channel_id=1, source_target_pairs={{2,0},{4,2},{6,4},{8,6},{10,8},{12,10},{14,12},{16,14},{18,16},{20... | collective-permute-start | bytes 1179656 | tf_op jit(solution)/shard_map/ppermute | solution.py:202
  46.7 9.7 %collective-permute-start.10 = (bf16[128,1536]{1,0:T(8,128)(2,1)S(1)}, bf16[128,1536]{1,0:T(8,128)(2,1)S(1)}, u32[]{:S(2)}, u32[]{:S(2)}) collective-permute-start(bf16[128,1536]{1,0:T(8,128)(2,1)S(1)} %get-tuple-element.25.refs_1_), channel_id=1, source_target_pairs={{0,1},{1,0},{2,3},{3,2},{4,5},{5,4},{6,7},{7,6},{8,9},{9,8},{10,11... | collective-permute-start | bytes 1179656 | tf_op jit(solution)/shard_map/ppermute | solution.py:205
  48.7 7.7 %collective-permute-start.11 = (bf16[128,1536]{1,0:T(8,128)(2,1)S(1)}, bf16[128,1536]{1,0:T(8,128)(2,1)S(1)}, u32[]{:S(2)}, u32[]{:S(2)}) collective-permute-start(bf16[128,1536]{1,0:T(8,128)(2,1)S(1)} %get-tuple-element.26.refs_2_), channel_id=1, source_target_pairs={{0,1},{1,0},{2,3},{3,2},{4,5},{5,4},{6,7},{7,6},{8,9},{9,8},{10,11... | collective-permute-start | bytes 1179656 | tf_op jit(solution)/shard_map/ppermute | solution.py:205
  48.8 7.6 %collective-permute-start.9 = (bf16[128,1536]{1,0:T(8,128)(2,1)S(1)}, bf16[128,1536]{1,0:T(8,128)(2,1)S(1)}, u32[]{:S(2)}, u32[]{:S(2)}) collective-permute-start(bf16[128,1536]{1,0:T(8,128)(2,1)S(1)} %get-tuple-element.24.refs_0_), channel_id=1, source_target_pairs={{0,1},{1,0},{2,3},{3,2},{4,5},{5,4},{6,7},{7,6},{8,9},{9,8},{10,11... | collective-permute-start | bytes 1179656 | tf_op jit(solution)/shard_map/ppermute | solution.py:205
  49.2 16.1 %collective-permute-start.7 = (bf16[128,1536]{1,0:T(8,128)(2,1)S(1)}, bf16[128,1536]{1,0:T(8,128)(2,1)S(1)}, u32[]{:S(2)}, u32[]{:S(2)}) collective-permute-start(bf16[128,1536]{1,0:T(8,128)(2,1)S(1)} %collective-permute-done.6.refs_3_), channel_id=1, source_target_pairs={{254,0},{0,2},{2,4},{4,6},{6,8},{8,10},{10,12},{12,14},{14,16},{16... | collective-permute-start | bytes 1179656 | tf_op jit(solution)/shard_map/ppermute | solution.py:202
  49.2 16.1 %collective-permute-start.8 = (bf16[128,1536]{1,0:T(8,128)(2,1)S(1)}, bf16[128,1536]{1,0:T(8,128)(2,1)S(1)}, u32[]{:S(2)}, u32[]{:S(2)}) collective-permute-start(bf16[128,1536]{1,0:T(8,128)(2,1)S(1)} %collective-permute-done.4.refs_0_), channel_id=1, source_target_pairs={{2,0},{4,2},{6,4},{8,6},{10,8},{12,10},{14,12},{16,14},{18,16},{20... | collective-permute-start | bytes 1179656 | tf_op jit(solution)/shard_map/ppermute | solution.py:202
  66.2 3.5 %collective-permute-start.12 = (bf16[128,1536]{1,0:T(8,128)(2,1)S(1)}, bf16[128,1536]{1,0:T(8,128)(2,1)S(1)}, u32[]{:S(2)}, u32[]{:S(2)}) collective-permute-start(bf16[128,1536]{1,0:T(8,128)(2,1)S(1)} %get-tuple-element.31.refs_0_), channel_id=1, source_target_pairs={{0,1},{1,0},{2,3},{3,2},{4,5},{5,4},{6,7},{7,6},{8,9},{9,8},{10,11... | collective-permute-start | bytes 1179656 | tf_op jit(solution)/shard_map/ppermute | solution.py:205
  68.3 1.9 %collective-permute-start.13 = (bf16[128,1536]{1,0:T(8,128)(2,1)S(1)}, bf16[128,1536]{1,0:T(8,128)(2,1)S(1)}, u32[]{:S(2)}, u32[]{:S(2)}) collective-permute-start(bf16[128,1536]{1,0:T(8,128)(2,1)S(1)} %get-tuple-element.32.refs_1_), channel_id=1, source_target_pairs={{0,1},{1,0},{2,3},{3,2},{4,5},{5,4},{6,7},{7,6},{8,9},{9,8},{10,11... | collective-permute-start | bytes 1179656 | tf_op jit(solution)/shard_map/ppermute | solution.py:205
  68.4 2.4 %collective-permute-start.14 = (bf16[128,1536]{1,0:T(8,128)(2,1)S(1)}, bf16[128,1536]{1,0:T(8,128)(2,1)S(1)}, u32[]{:S(2)}, u32[]{:S(2)}) collective-permute-start(bf16[128,1536]{1,0:T(8,128)(2,1)S(1)} %get-tuple-element.33.refs_2_), channel_id=1, source_target_pairs={{0,1},{1,0},{2,3},{3,2},{4,5},{5,4},{6,7},{7,6},{8,9},{9,8},{10,11... | collective-permute-start | bytes 1179656 | tf_op jit(solution)/shard_map/ppermute | solution.py:205

commit v3 on v2

--- a/solution.py
+++ b/solution.py
@@ -71,22 +71,17 @@
 
 
 def fill_columns(own, other, columns):
-    count = columns.shape[0] // 2
-    at = 0
-    for pair in zip(own, other):
-        size, samples = pair[0].shape
-        low, high = pl.ds(at, size), pl.ds(count + at, size)
-        lane = lax.broadcasted_iota(jnp.int32, (size, EDGE), 1)
-        edge = jnp.zeros((size, EDGE), jnp.float32)
-        for g, target in enumerate(pair):
-            block = target[...]
-            columns[low, g * samples : (g + 1) * samples] = block
-            ahead = jnp.concatenate([block[:, 1:], jnp.zeros((size, 1), block.dtype)], 1)
-            columns[high, g * samples : (g + 1) * samples] = ahead
-            edge = jnp.where(lane == g, block[:, :EDGE].astype(jnp.float32)[:, :1], edge)
-        columns[low, 2 * samples :] = jnp.zeros((size, EDGE), jnp.bfloat16)
-        columns[high, 2 * samples :] = edge.astype(jnp.bfloat16)
-        at += size
+    count, samples = own.shape
+    lane = lax.broadcasted_iota(jnp.int32, (count, EDGE), 1)
+    edge = jnp.zeros((count, EDGE), jnp.float32)
+    for g, target in enumerate((own, other)):
+        block = target[...]
+        columns[:count, g * samples : (g + 1) * samples] = block
+        ahead = jnp.concatenate([block[:, 1:], jnp.zeros((count, 1), block.dtype)], 1)
+        columns[count:, g * samples : (g + 1) * samples] = ahead
+        edge = jnp.where(lane == g, block[:, :EDGE].astype(jnp.float32)[:, :1], edge)
+    columns[:count, 2 * samples :] = jnp.zeros((count, EDGE), jnp.bfloat16)
+    columns[count:, 2 * samples :] = edge.astype(jnp.bfloat16)
 
 
 def is_in(distance, distances):
@@ -96,10 +91,9 @@
     return found
 
 
-def pick_kernel(distances, counts, wanted, *refs):
-    n = sum(counts)
-    parts, outs, sem = list(refs[:n]), refs[n:-1], refs[-1]
-    blocks = [[parts.pop(0) for _ in range(c)] for c in counts]
+def pick_kernel(distances, wanted, *refs):
+    n = len(distances)
+    blocks, outs, sem = refs[:n], refs[n:-1], refs[-1]
 
     for action in ("start", "wait"):
         for slot in range(P_MAX):
@@ -107,74 +101,77 @@
 
                 @pl.when(wanted[slot] == d)
                 def _(slot=slot, block=block):
-                    size = block[0].shape[0]
-                    for h, part in enumerate(block):
-                        copy = pltpu.make_async_copy(part, outs[slot].at[pl.ds(h * size, size)], sem)
-                        copy.start() if action == "start" else copy.wait()
+                    copy = pltpu.make_async_copy(block, outs[slot], sem)
+                    copy.start() if action == "start" else copy.wait()
 
 
 def pick(distances, wanted, blocks):
-    counts = [len(block) for block in blocks]
-    size, samples = blocks[0][0].shape
-    shape = jax.ShapeDtypeStruct((size * counts[0], samples), jnp.bfloat16)
-    parts = [part for block in blocks for part in block]
+    shape = jax.ShapeDtypeStruct(blocks[0].shape, jnp.bfloat16)
     picked = pl.pallas_call(
-        functools.partial(pick_kernel, distances, counts),
+        functools.partial(pick_kernel, distances),
         out_shape=[shape] * P_MAX,
-        in_specs=[SMEM] + [ANY] * len(parts),
+        in_specs=[SMEM] + [ANY] * len(blocks),
         out_specs=[ANY] * P_MAX,
         scratch_shapes=[pltpu.SemaphoreType.DMA],
         compiler_params=pltpu.CompilerParams(vmem_limit_bytes=8 * 2**20),
         cost_estimate=FREE,
         name="pick",
-    )(wanted, *parts)
+    )(wanted, *blocks)
     return list(picked)
 
 
-def tile_kernel(distances, wanted, rows, *refs):
-    own, other = refs[:P_MAX], refs[P_MAX : 2 * P_MAX]
+def tile_kernel(distances, by_slot, wanted, rows, *refs):
+    n = P_MAX if by_slot else len(distances)
+    own, other = refs[:n], refs[n : 2 * n]
     out, columns, tile, sem = refs[-4:]
     count = columns.shape[0] // 2
     half = rows.shape[0] // PAIRS
+
+    def send(slot):
+        return pltpu.make_async_copy(tile.at[slot], out.at[0, slot], sem.at[slot])
 
     @pl.loop(0, P_MAX)
     def _(slot):
         @pl.when(is_in(wanted[slot], distances))
         def _():
-            for k in range(P_MAX):
-
-                @pl.when(slot == k)
+            for k in range(n):
+
+                @pl.when(slot == k if by_slot else wanted[slot] == distances[k])
                 def _(k=k):
-                    fill_columns(own[k : k + 1], other[k : k + 1], columns)
+                    fill_columns(own[k], other[k], columns)
 
             got = lax.dot_general(
                 rows[...], columns[...], (((1,), (1,)), ((), ())), preferred_element_type=jnp.float32
             )
             for m in range(PAIRS):
                 part = got[m * half : (m + 1) * half]
-                tile[2 * m] = part[:, :count]
+                tile[slot, 2 * m] = part[:, :count]
                 if 2 * m + 1 < LAGS:
-                    tile[2 * m + 1] = part[:, count:]
-            copy = pltpu.make_async_copy(tile, out.at[0, slot], sem)
-            copy.start()
-            copy.wait()
-
-
-def tiles(distances, wanted, stacked, own, other, so_far):
+                    tile[slot, 2 * m + 1] = part[:, count:]
+            send(slot).start()
+
+    @pl.loop(0, P_MAX)
+    def _(slot):
+        @pl.when(is_in(wanted[slot], distances))
+        def _():
+            send(slot).wait()
+
+
+def tiles(distances, wanted, stacked, own, other, so_far, by_slot=False):
     rows = stacked.shape
     half = rows[0] // PAIRS
     count = 2 * half
     stacked = pltpu.with_memory_space_constraint(stacked, pltpu.VMEM)
     arguments = [wanted, stacked, *own, *other, so_far]
     return pl.pallas_call(
-        functools.partial(tile_kernel, distances),
+        functools.partial(tile_kernel, distances, by_slot),
         out_shape=jax.ShapeDtypeStruct(so_far.shape, so_far.dtype),
         in_specs=[SMEM] + [VMEM] * (len(arguments) - 2) + [ANY],
         out_specs=ANY,
         scratch_shapes=[
             pltpu.VMEM((2 * count, rows[1]), jnp.bfloat16),
-            pltpu.VMEM((LAGS, half, count), jnp.float32),
-            pltpu.SemaphoreType.DMA,
+            pltpu.VMEM((P_MAX, LAGS, half, count), jnp.float32),
+            pltpu.SemaphoreType.DMA((P_MAX,)),
         ],
         input_output_aliases={len(arguments) - 1: 0},
         compiler_params=pltpu.CompilerParams(vmem_limit_bytes=16 * 2**20),
@@ -209,22 +206,23 @@
 
     mine = lax.dynamic_slice_in_dim(own, core * half, half, 0)
     theirs = lax.dynamic_slice_in_dim(own, (1 - core) * half, half, 0)
-    d1 = move([own], down)
-    below = move([own], next_row)
+    d1 = move([own], down)[0]
+    below = move([own], next_row)[0]
+    before = move([own], turn)[0]
     theirs = swap([theirs])[0]
+    below, before, theirs = step(below, before, theirs)
+    d7 = move([below], turn)[0]
+    d2 = move([d1], down[:-1])[0]
     rows, result = stack(wanted, mine, theirs)
-    below, rows, result = step(below, rows, result)
-    d7 = move(below, turn)
-    d2 = move(d1, down)
-    d6 = move(d7, up)
-    d3 = move(d2, down)
-    d5 = move(d6, up)
-    d4 = move(d3, down)
+    d7, rows, result = step(d7, rows, result)
+    d6 = move([jnp.where(me % row == row - 1, before, d7)], turn)[0]
+    d3 = move([d2], down)[0]
+    d5 = move([d6], up)[0]
+    d4 = move([d3], down)[0]
     near = pick((1, 7, 2, 6), wanted, [d1, d7, d2, d6])
-    result = tiles((1, 7, 2, 6), wanted, rows, near, swap(near), result)
-    d3, d5, d4, result = step(d3, d5, d4, result)
-    far = pick((3, 5, 4), wanted, [d3, d5, d4])
-    return tiles((3, 5, 4), wanted, rows, far, swap(far), result)
+    result = tiles((1, 7, 2, 6), wanted, rows, near, swap(near), result, True)
+    d3, d5, result = step(d3, d5, result)
+    return tiles((3, 5, 4), wanted, rows, [d3, d5, d4], swap([d3, d5, d4]), result)
 
 
 def solution(mesh):

time: 75 us -> 72.5 us (0.967)
  starting transfers between devices: 41.3 us -> 36 us
  waiting for transfers between devices: 15.3 us -> 19.5 us
  Pallas kernels: 15.7 us -> 13.8 us
    ppermute x8 -> x9, starting transfers between devices: 35.1 us -> 28.8 us  [move(): return [lax.ppermute(p, 'chan', route) for p in parts]]
    ppermute x8 -> x9, waiting for transfers between devices: 13.3 us -> 18.1 us  [move(): return [lax.ppermute(p, 'chan', route) for p in parts]]
    pallas_call x4 -> x3, Pallas kernels: 13.2 us -> 11.2 us  [the longest x2 10.3 us: tiles(): pl.pallas_call(functools.partial(tile_kernel, distances, by_slot), out_sh...]
    ppermute x7, starting transfers between devices: 6.17 us -> 7.21 us  [swap(): return [lax.ppermute(p, 'tm', [(0, 1), (1, 0)]) for p in parts]]
  transfers between devices with their start and end apart: 15 -> 16, of which waited for: 8 -> 9; matrix products, arithmetic and copies ran while one was open for 2% -> 2% of each run, Pallas kernels for 15% -> 10%
where the time goes in v3:
time: 72.5 us; the launch traced here: 71.9 us
  starting transfers between devices  36 us (50%)
  waiting for transfers between devices  19.5 us (27%)
  Pallas kernels  13.8 us (19%)
  local copies, waits for them, and re-layouts  1.05 us (1%)
  between operations  0.89 us (1%)
    ppermute x9, starting transfers between devices, move(): return [lax.ppermute(p, 'chan', route) for p in parts]  28.8 us
    ppermute x9, waiting for transfers between devices, move(): return [lax.ppermute(p, 'chan', route) for p in parts]  18.1 us
    pallas_call x2, Pallas kernels, tiles(): pl.pallas_call(functools.partial(tile_kernel, distances, by_slot), out_sh...  10.3 us
    ppermute x7, starting transfers between devices, swap(): return [lax.ppermute(p, 'tm', [(0, 1), (1, 0)]) for p in parts]  7.21 us
    pallas_call x1, Pallas kernels, stack(): pl.pallas_call(stack_kernel, out_shape=[pltpu.VMEM((PAIRS * half, 2 * sam...  2.56 us
  transfers between devices with their start and end apart: 16, of which 9 were waited for; matrix products, arithmetic and copies ran while one was open for 2% of the time, Pallas kernels for 10%

profile of v3, /device:TPU:1, one launch (start us, length us, event | category | flops | bytes accessed | tf_op | source)
XLA Modules:
  0.0 71.9 jit_solution(14092818647661769901)
XLA Ops:
  0.0 7.7 %collective-permute-start = (bf16[128,1536]{1,0:T(8,128)(2,1)}, bf16[128,1536]{1,0:T(8,128)(2,1)S(1)}, u32[]{:S(2)}, u32[]{:S(2)}) collective-permute-start(bf16[128,1536]{1,0:T(8,128)(2,1)} %bitcast.9), channel_id=1, source_target_pairs={{16,0},{18,2},{20,4},{22,6},{24,8},{26,10},{28,12},{14,14},{32,16}... | collective-permute-start | bytes 1179656 | tf_op jit(solution)/shard_map/ppermute | solution.py:199
  7.7 1.7 %collective-permute-start.1 = (bf16[128,1536]{1,0:T(8,128)(2,1)}, bf16[128,1536]{1,0:T(8,128)(2,1)S(1)}, u32[]{:S(2)}, u32[]{:S(2)}) collective-permute-start(bf16[128,1536]{1,0:T(8,128)(2,1)} %bitcast.10), channel_id=1, source_target_pairs={{14,0},{0,2},{2,4},{4,6},{6,8},{8,10},{10,12},{12,14},{30,16},{16,... | collective-permute-start | bytes 1179656 | tf_op jit(solution)/shard_map/ppermute | solution.py:199
  9.4 1.0 %dynamic-slice_bitcast_fusion = (bf16[64,1536]{1,0:T(8,128)(2,1)S(1)}, bf16[64,1536]{1,0:T(8,128)(2,1)S(1)}) fusion(bf16[1,1,128,1536]{3,2,1,0:T(8,128)(2,1)} %param.3, s32[]{:T(128)S(6)} %select_n.27, s32[]{:T(128)S(6)} %select_n.26), kind=kLoop, calls=%fused_computation.1 | loop fusion | bytes 786440 | tf_op jit(solution)/shard_map/dynamic_slice | solution.py:207
  10.4 1.3 %collective-permute-start.2 = (bf16[64,1536]{1,0:T(8,128)(2,1)S(1)}, bf16[64,1536]{1,0:T(8,128)(2,1)S(1)}, u32[]{:S(2)}, u32[]{:S(2)}) collective-permute-start(bf16[64,1536]{1,0:T(8,128)(2,1)S(1)} %get-tuple-element.34), channel_id=1, source_target_pairs={{0,1},{1,0},{2,3},{3,2},{4,5},{5,4},{6,7},{7,6},{8,9},{9,8},{10,11... | collective-permute-start | bytes 589832 | tf_op jit(solution)/shard_map/ppermute | solution.py:202
  11.8 2.8 %collective-permute-start.4 = (bf16[128,1536]{1,0:T(8,128)(2,1)}, bf16[128,1536]{1,0:T(8,128)(2,1)S(1)}, u32[]{:S(2)}, u32[]{:S(2)}) collective-permute-start(bf16[128,1536]{1,0:T(8,128)(2,1)} %bitcast.11), channel_id=1, source_target_pairs={{2,0},{4,2},{6,4},{8,6},{10,8},{12,10},{14,12},{16,14},{18,16},{20... | collective-permute-start | bytes 1179656 | tf_op jit(solution)/shard_map/ppermute | solution.py:199
  14.5 1.2 %collective-permute-done = bf16[128,1536]{1,0:T(8,128)(2,1)S(1)} collective-permute-done((bf16[128,1536]{1,0:T(8,128)(2,1)}, bf16[128,1536]{1,0:T(8,128)(2,1)S(1)}, u32[]{:S(2)}, u32[]{:S(2)}) %collective-permute-start) | collective-permute-done | bytes 393248 | tf_op jit(solution)/shard_map/ppermute | solution.py:199
  15.7 3.1 %collective-permute-done.1 = bf16[128,1536]{1,0:T(8,128)(2,1)S(1)} collective-permute-done((bf16[128,1536]{1,0:T(8,128)(2,1)}, bf16[128,1536]{1,0:T(8,128)(2,1)S(1)}, u32[]{:S(2)}, u32[]{:S(2)}) %collective-permute-start.1) | collective-permute-done | bytes 393248 | tf_op jit(solution)/shard_map/ppermute | solution.py:199
  18.8 0.4 collective-permute-start.3
  19.9 0.7 compare_select_fusion.wanted
  20.6 2.6 %stack.1 = (bf16[1088,3200]{1,0:T(8,128)(2,1)S(1)}, f32[1,3,33,64,128]{4,3,2,1,0:T(8,128)}) custom-call(s32[3]{0:T(128)S(1)} %compare_select_fusion.wanted, bf16[64,1536]{1,0:T(8,128)(2,1)S(1)} %get-tuple-element.33.first, bf16[64,1536]{1,0:T(8,128)(2,1)S(1)} %collective-permute-done.2.second), custom_call_target="tpu_custom_call" | custom-call | tf_op jit(solution)/shard_map/stack/pallas_call | solution.py:54
  23.3 1.3 %collective-permute-start.5 = (bf16[128,1536]{1,0:T(8,128)(2,1)S(1)}, bf16[128,1536]{1,0:T(8,128)(2,1)S(1)}, u32[]{:S(2)}, u32[]{:S(2)}) collective-permute-start(bf16[128,1536]{1,0:T(8,128)(2,1)S(1)} %collective-permute-done.4.refs_0_), channel_id=1, source_target_pairs={{2,0},{4,2},{6,4},{8,6},{10,8},{12,10},{14,12},{16,14},{18,16},{20... | collective-permute-start | bytes 1179656 | tf_op jit(solution)/shard_map/ppermute | solution.py:199
  24.6 6.1 %collective-permute-done.3.refs_1_ = bf16[128,1536]{1,0:T(8,128)(2,1)S(1)} collective-permute-done((bf16[128,1536]{1,0:T(8,128)(2,1)S(1)}, bf16[128,1536]{1,0:T(8,128)(2,1)S(1)}, u32[]{:S(2)}, u32[]{:S(2)}) %collective-permute-start.3) | collective-permute-done | bytes 393248 | tf_op jit(solution)/shard_map/ppermute | solution.py:199
  30.8 3.1 %collective-permute-done.5.refs_2_ = bf16[128,1536]{1,0:T(8,128)(2,1)S(1)} collective-permute-done((bf16[128,1536]{1,0:T(8,128)(2,1)S(1)}, bf16[128,1536]{1,0:T(8,128)(2,1)S(1)}, u32[]{:S(2)}, u32[]{:S(2)}) %collective-permute-start.5) | collective-permute-done | bytes 393248 | tf_op jit(solution)/shard_map/ppermute | solution.py:199
  33.9 7.2 %collective-permute-start.6 = (bf16[128,1536]{1,0:T(8,128)(2,1)S(1)}, bf16[128,1536]{1,0:T(8,128)(2,1)S(1)}, u32[]{:S(2)}, u32[]{:S(2)}) collective-permute-start(bf16[128,1536]{1,0:T(8,128)(2,1)S(1)} %collective-permute-done.5.refs_2_), channel_id=1, source_target_pairs={{2,0},{4,2},{6,4},{8,6},{10,8},{12,10},{14,12},{16,14},{18,16},{20... | collective-permute-start | bytes 1179656 | tf_op jit(solution)/shard_map/ppermute | solution.py:199
  41.1 0.9 %pick.1 = (bf16[128,1536]{1,0:T(8,128)(2,1)S(1)}, bf16[128,1536]{1,0:T(8,128)(2,1)S(1)}, bf16[128,1536]{1,0:T(8,128)(2,1)S(1)}) custom-call(s32[3]{0:T(128)S(1)} %compare_select_fusion.wanted, bf16[128,1536]{1,0:T(8,128)(2,1)S(1)} %collective-permute-done.4.refs_0_, bf16[128,1536]{1,0:T(8,128)(2,1)S(1)} %collective-permute-done.3.refs_1_, ...), custom_call_target="tpu_custom_call" | custom-call | tf_op jit(solution)/shard_map/pick/pallas_call | solution.py:110
  42.0 2.8 %collective-permute-start.10 = (bf16[128,1536]{1,0:T(8,128)(2,1)S(1)}, bf16[128,1536]{1,0:T(8,128)(2,1)S(1)}, u32[]{:S(2)}, u32[]{:S(2)}) collective-permute-start(bf16[128,1536]{1,0:T(8,128)(2,1)S(1)} %get-tuple-element.27.refs_1_), channel_id=1, source_target_pairs={{0,1},{1,0},{2,3},{3,2},{4,5},{5,4},{6,7},{7,6},{8,9},{9,8},{10,11... | collective-permute-start | bytes 1179656 | tf_op jit(solution)/shard_map/ppermute | solution.py:202
  45.4 1.7 %collective-permute-done.6.refs_0_ = bf16[128,1536]{1,0:T(8,128)(2,1)S(1)} collective-permute-done((bf16[128,1536]{1,0:T(8,128)(2,1)S(1)}, bf16[128,1536]{1,0:T(8,128)(2,1)S(1)}, u32[]{:S(2)}, u32[]{:S(2)}) %collective-permute-start.6) | collective-permute-done | bytes 393248 | tf_op jit(solution)/shard_map/ppermute | solution.py:199
  47.1 7.6 %collective-permute-start.12 = (bf16[128,1536]{1,0:T(8,128)(2,1)S(1)}, bf16[128,1536]{1,0:T(8,128)(2,1)S(1)}, u32[]{:S(2)}, u32[]{:S(2)}) collective-permute-start(bf16[128,1536]{1,0:T(8,128)(2,1)S(1)} %collective-permute-done.6.refs_0_), channel_id=1, source_target_pairs={{2,0},{4,2},{6,4},{8,6},{10,8},{12,10},{14,12},{16,14},{18,16},{20... | collective-permute-start | bytes 1179656 | tf_op jit(solution)/shard_map/ppermute | solution.py:199
  54.7 3.9 %tiles_1_7_2_6.1.refs_6_ = f32[1,3,33,64,128]{4,3,2,1,0:T(8,128)} custom-call(s32[3]{0:T(128)S(1)} %compare_select_fusion.wanted, bf16[1088,3200]{1,0:T(8,128)(2,1)S(1)} %get-tuple-element.23.rows, bf16[128,1536]{1,0:T(8,128)(2,1)S(1)} %get-tuple-element.26.refs_0_, bf16[128,1536]{1,0:T(8,128)(2,1)S(1)} %get-tuple-element.27.refs_1_, ...), custom_call_target="tpu_custom_call", output_to_operand_aliasing={{}: (8, {})} | custom-call | tf_op jit(solution)/shard_map/tiles_1_7_2_6/pallas_call | solution.py:166
  58.7 2.8 %collective-permute-done.8.refs_1_ = bf16[128,1536]{1,0:T(8,128)(2,1)S(1)} collective-permute-done((bf16[128,1536]{1,0:T(8,128)(2,1)S(1)}, bf16[128,1536]{1,0:T(8,128)(2,1)S(1)}, u32[]{:S(2)}, u32[]{:S(2)}) %collective-permute-start.8) | collective-permute-done | bytes 393248 | tf_op jit(solution)/shard_map/ppermute | solution.py:199
  61.5 1.0 %collective-permute-start.13 = (bf16[128,1536]{1,0:T(8,128)(2,1)S(1)}, bf16[128,1536]{1,0:T(8,128)(2,1)S(1)}, u32[]{:S(2)}, u32[]{:S(2)}) collective-permute-start(bf16[128,1536]{1,0:T(8,128)(2,1)S(1)} %collective-permute-done.6.refs_0_), channel_id=1, source_target_pairs={{0,1},{1,0},{2,3},{3,2},{4,5},{5,4},{6,7},{7,6},{8,9},{9,8},{10,11... | collective-permute-start | bytes 1179656 | tf_op jit(solution)/shard_map/ppermute | solution.py:202
  62.5 1.5 %collective-permute-start.15 = (bf16[128,1536]{1,0:T(8,128)(2,1)S(1)}, bf16[128,1536]{1,0:T(8,128)(2,1)S(1)}, u32[]{:S(2)}, u32[]{:S(2)}) collective-permute-start(bf16[128,1536]{1,0:T(8,128)(2,1)S(1)} %collective-permute-done.12.refs_2_), channel_id=1, source_target_pairs={{0,1},{1,0},{2,3},{3,2},{4,5},{5,4},{6,7},{7,6},{8,9},{9,8},{10,11... | collective-permute-start | bytes 1179656 | tf_op jit(solution)/shard_map/ppermute | solution.py:202
  64.3 1.0 %collective-permute-done.15.refs_5_ = bf16[128,1536]{1,0:T(8,128)(2,1)S(1)} collective-permute-done((bf16[128,1536]{1,0:T(8,128)(2,1)S(1)}, bf16[128,1536]{1,0:T(8,128)(2,1)S(1)}, u32[]{:S(2)}, u32[]{:S(2)}) %collective-permute-start.15) | collective-permute-done | bytes 393248 | tf_op jit(solution)/shard_map/ppermute | solution.py:202
  65.4 6.4 %tiles_3_5_4.1 = f32[1,3,33,64,128]{4,3,2,1,0:T(8,128)} custom-call(s32[3]{0:T(128)S(1)} %compare_select_fusion.wanted, bf16[1088,3200]{1,0:T(8,128)(2,1)S(1)} %get-tuple-element.23.rows, bf16[128,1536]{1,0:T(8,128)(2,1)S(1)} %collective-permute-done.6.refs_0_, bf16[128,1536]{1,0:T(8,128)(2,1)S(1)} %collective-permute-done.8.refs_1_, ...), custom_call_target="tpu_custom_call", output_to_operand_aliasing={{}: (8, {})} | custom-call | tf_op jit(solution)/shard_map/tiles_3_5_4/pallas_call | solution.py:166
  (15 shorter events, 1.2 us)
Async XLA Ops:
  0.0 15.7 %collective-permute-start = (bf16[128,1536]{1,0:T(8,128)(2,1)}, bf16[128,1536]{1,0:T(8,128)(2,1)S(1)}, u32[]{:S(2)}, u32[]{:S(2)}) collective-permute-start(bf16[128,1536]{1,0:T(8,128)(2,1)} %bitcast.9), channel_id=1, source_target_pairs={{16,0},{18,2},{20,4},{22,6},{24,8},{26,10},{28,12},{14,14},{32,16}... | collective-permute-start | bytes 1179656 | tf_op jit(solution)/shard_map/ppermute | solution.py:199
  7.7 11.2 %collective-permute-start.1 = (bf16[128,1536]{1,0:T(8,128)(2,1)}, bf16[128,1536]{1,0:T(8,128)(2,1)S(1)}, u32[]{:S(2)}, u32[]{:S(2)}) collective-permute-start(bf16[128,1536]{1,0:T(8,128)(2,1)} %bitcast.10), channel_id=1, source_target_pairs={{14,0},{0,2},{2,4},{4,6},{6,8},{8,10},{10,12},{12,14},{30,16},{16,... | collective-permute-start | bytes 1179656 | tf_op jit(solution)/shard_map/ppermute | solution.py:199
  10.4 4.1 %collective-permute-start.2 = (bf16[64,1536]{1,0:T(8,128)(2,1)S(1)}, bf16[64,1536]{1,0:T(8,128)(2,1)S(1)}, u32[]{:S(2)}, u32[]{:S(2)}) collective-permute-start(bf16[64,1536]{1,0:T(8,128)(2,1)S(1)} %get-tuple-element.34), channel_id=1, source_target_pairs={{0,1},{1,0},{2,3},{3,2},{4,5},{5,4},{6,7},{7,6},{8,9},{9,8},{10,11... | collective-permute-start | bytes 589832 | tf_op jit(solution)/shard_map/ppermute | solution.py:202
  11.8 11.6 %collective-permute-start.4 = (bf16[128,1536]{1,0:T(8,128)(2,1)}, bf16[128,1536]{1,0:T(8,128)(2,1)S(1)}, u32[]{:S(2)}, u32[]{:S(2)}) collective-permute-start(bf16[128,1536]{1,0:T(8,128)(2,1)} %bitcast.11), channel_id=1, source_target_pairs={{2,0},{4,2},{6,4},{8,6},{10,8},{12,10},{14,12},{16,14},{18,16},{20... | collective-permute-start | bytes 1179656 | tf_op jit(solution)/shard_map/ppermute | solution.py:199
  18.8 11.8 %collective-permute-start.3 = (bf16[128,1536]{1,0:T(8,128)(2,1)S(1)}, bf16[128,1536]{1,0:T(8,128)(2,1)S(1)}, u32[]{:S(2)}, u32[]{:S(2)}) collective-permute-start(bf16[128,1536]{1,0:T(8,128)(2,1)S(1)} %collective-permute-done), channel_id=1, source_target_pairs={{14,0},{0,2},{2,4},{4,6},{6,8},{8,10},{10,12},{12,14},{30,16},{16,... | collective-permute-start | bytes 1179656 | tf_op jit(solution)/shard_map/ppermute | solution.py:199
  23.3 10.6 %collective-permute-start.5 = (bf16[128,1536]{1,0:T(8,128)(2,1)S(1)}, bf16[128,1536]{1,0:T(8,128)(2,1)S(1)}, u32[]{:S(2)}, u32[]{:S(2)}) collective-permute-start(bf16[128,1536]{1,0:T(8,128)(2,1)S(1)} %collective-permute-done.4.refs_0_), channel_id=1, source_target_pairs={{2,0},{4,2},{6,4},{8,6},{10,8},{12,10},{14,12},{16,14},{18,16},{20... | collective-permute-start | bytes 1179656 | tf_op jit(solution)/shard_map/ppermute | solution.py:199
  30.7 10.4 %collective-permute-start.7 = (bf16[128,1536]{1,0:T(8,128)(2,1)S(1)}, bf16[128,1536]{1,0:T(8,128)(2,1)S(1)}, u32[]{:S(2)}, u32[]{:S(2)}) collective-permute-start(bf16[128,1536]{1,0:T(8,128)(2,1)S(1)} %broadcast_select_fusion), channel_id=1, source_target_pairs={{14,0},{0,2},{2,4},{4,6},{6,8},{8,10},{10,12},{12,14},{30,16},{16,... | collective-permute-start | bytes 1179656 | tf_op jit(solution)/shard_map/ppermute | solution.py:199
  33.9 13.2 %collective-permute-start.6 = (bf16[128,1536]{1,0:T(8,128)(2,1)S(1)}, bf16[128,1536]{1,0:T(8,128)(2,1)S(1)}, u32[]{:S(2)}, u32[]{:S(2)}) collective-permute-start(bf16[128,1536]{1,0:T(8,128)(2,1)S(1)} %collective-permute-done.5.refs_2_), channel_id=1, source_target_pairs={{2,0},{4,2},{6,4},{8,6},{10,8},{12,10},{14,12},{16,14},{18,16},{20... | collective-permute-start | bytes 1179656 | tf_op jit(solution)/shard_map/ppermute | solution.py:199
  42.0 12.7 %collective-permute-start.10 = (bf16[128,1536]{1,0:T(8,128)(2,1)S(1)}, bf16[128,1536]{1,0:T(8,128)(2,1)S(1)}, u32[]{:S(2)}, u32[]{:S(2)}) collective-permute-start(bf16[128,1536]{1,0:T(8,128)(2,1)S(1)} %get-tuple-element.27.refs_1_), channel_id=1, source_target_pairs={{0,1},{1,0},{2,3},{3,2},{4,5},{5,4},{6,7},{7,6},{8,9},{9,8},{10,11... | collective-permute-start | bytes 1179656 | tf_op jit(solution)/shard_map/ppermute | solution.py:202
  44.9 9.8 %collective-permute-start.11 = (bf16[128,1536]{1,0:T(8,128)(2,1)S(1)}, bf16[128,1536]{1,0:T(8,128)(2,1)S(1)}, u32[]{:S(2)}, u32[]{:S(2)}) collective-permute-start(bf16[128,1536]{1,0:T(8,128)(2,1)S(1)} %get-tuple-element.28.refs_2_), channel_id=1, source_target_pairs={{0,1},{1,0},{2,3},{3,2},{4,5},{5,4},{6,7},{7,6},{8,9},{9,8},{10,11... | collective-permute-start | bytes 1179656 | tf_op jit(solution)/shard_map/ppermute | solution.py:202
  45.0 9.7 %collective-permute-start.9 = (bf16[128,1536]{1,0:T(8,128)(2,1)S(1)}, bf16[128,1536]{1,0:T(8,128)(2,1)S(1)}, u32[]{:S(2)}, u32[]{:S(2)}) collective-permute-start(bf16[128,1536]{1,0:T(8,128)(2,1)S(1)} %get-tuple-element.26.refs_0_), channel_id=1, source_target_pairs={{0,1},{1,0},{2,3},{3,2},{4,5},{5,4},{6,7},{7,6},{8,9},{9,8},{10,11... | collective-permute-start | bytes 1179656 | tf_op jit(solution)/shard_map/ppermute | solution.py:202
  45.4 16.1 %collective-permute-start.8 = (bf16[128,1536]{1,0:T(8,128)(2,1)S(1)}, bf16[128,1536]{1,0:T(8,128)(2,1)S(1)}, u32[]{:S(2)}, u32[]{:S(2)}) collective-permute-start(bf16[128,1536]{1,0:T(8,128)(2,1)S(1)} %collective-permute-done.7.refs_3_), channel_id=1, source_target_pairs={{254,0},{0,2},{2,4},{4,6},{6,8},{8,10},{10,12},{12,14},{14,16},{16... | collective-permute-start | bytes 1179656 | tf_op jit(solution)/shard_map/ppermute | solution.py:199
  47.1 15.5 %collective-permute-start.12 = (bf16[128,1536]{1,0:T(8,128)(2,1)S(1)}, bf16[128,1536]{1,0:T(8,128)(2,1)S(1)}, u32[]{:S(2)}, u32[]{:S(2)}) collective-permute-start(bf16[128,1536]{1,0:T(8,128)(2,1)S(1)} %collective-permute-done.6.refs_0_), channel_id=1, source_target_pairs={{2,0},{4,2},{6,4},{8,6},{10,8},{12,10},{14,12},{16,14},{18,16},{20... | collective-permute-start | bytes 1179656 | tf_op jit(solution)/shard_map/ppermute | solution.py:199
  61.5 2.6 %collective-permute-start.13 = (bf16[128,1536]{1,0:T(8,128)(2,1)S(1)}, bf16[128,1536]{1,0:T(8,128)(2,1)S(1)}, u32[]{:S(2)}, u32[]{:S(2)}) collective-permute-start(bf16[128,1536]{1,0:T(8,128)(2,1)S(1)} %collective-permute-done.6.refs_0_), channel_id=1, source_target_pairs={{0,1},{1,0},{2,3},{3,2},{4,5},{5,4},{6,7},{7,6},{8,9},{9,8},{10,11... | collective-permute-start | bytes 1179656 | tf_op jit(solution)/shard_map/ppermute | solution.py:202
  62.4 1.9 %collective-permute-start.14 = (bf16[128,1536]{1,0:T(8,128)(2,1)S(1)}, bf16[128,1536]{1,0:T(8,128)(2,1)S(1)}, u32[]{:S(2)}, u32[]{:S(2)}) collective-permute-start(bf16[128,1536]{1,0:T(8,128)(2,1)S(1)} %collective-permute-done.8.refs_1_), channel_id=1, source_target_pairs={{0,1},{1,0},{2,3},{3,2},{4,5},{5,4},{6,7},{7,6},{8,9},{9,8},{10,11... | collective-permute-start | bytes 1179656 | tf_op jit(solution)/shard_map/ppermute | solution.py:202
  62.5 2.8 %collective-permute-start.15 = (bf16[128,1536]{1,0:T(8,128)(2,1)S(1)}, bf16[128,1536]{1,0:T(8,128)(2,1)S(1)}, u32[]{:S(2)}, u32[]{:S(2)}) collective-permute-start(bf16[128,1536]{1,0:T(8,128)(2,1)S(1)} %collective-permute-done.12.refs_2_), channel_id=1, source_target_pairs={{0,1},{1,0},{2,3},{3,2},{4,5},{5,4},{6,7},{7,6},{8,9},{9,8},{10,11... | collective-permute-start | bytes 1179656 | tf_op jit(solution)/shard_map/ppermute | solution.py:202

commit v4 on v3

--- a/solution.py
+++ b/solution.py
@@ -210,7 +210,7 @@
     below = move([own], next_row)[0]
     before = move([own], turn)[0]
     theirs = swap([theirs])[0]
-    below, before, theirs = step(below, before, theirs)
+    below, before, theirs, d1 = step(below, before, theirs, d1)
     d7 = move([below], turn)[0]
     d2 = move([d1], down[:-1])[0]
     rows, result = stack(wanted, mine, theirs)
@@ -221,7 +221,7 @@
     d4 = move([d3], down)[0]
     near = pick((1, 7, 2, 6), wanted, [d1, d7, d2, d6])
     result = tiles((1, 7, 2, 6), wanted, rows, near, swap(near), result, True)
-    d3, d5, result = step(d3, d5, result)
+    d5, result = step(d5, result)
     return tiles((3, 5, 4), wanted, rows, [d3, d5, d4], swap([d3, d5, d4]), result)
 
 

time: 72.5 us -> 70.7 us (0.975)
  waiting for transfers between devices: 19.5 us -> 16.9 us
    ppermute x9, waiting for transfers between devices: 18.1 us -> 14 us  [move(): return [lax.ppermute(p, 'chan', route) for p in parts]]
    ppermute x7, starting transfers between devices: 7.21 us -> 9.57 us  [swap(): return [lax.ppermute(p, 'tm', [(0, 1), (1, 0)]) for p in parts]]
    ppermute x9, starting transfers between devices: 28.8 us -> 26.6 us  [move(): return [lax.ppermute(p, 'chan', route) for p in parts]]
    ppermute x7, waiting for transfers between devices: 1.36 us -> 2.85 us  [swap(): return [lax.ppermute(p, 'tm', [(0, 1), (1, 0)]) for p in parts]]
  transfers between devices with their start and end apart: 16 -> 16, of which waited for: 9 -> 8; matrix products, arithmetic and copies ran while one was open for 2% -> 3% of each run, Pallas kernels for 10% -> 14%
where the time goes in v4:
time: 70.7 us; the launch traced here: 69.7 us
  starting transfers between devices  36.2 us (51%)
  waiting for transfers between devices  16.9 us (24%)
  Pallas kernels  13.9 us (20%)
  local copies, waits for them, and re-layouts  1.05 us (1%)
  between operations  0.9 us (1%)
    ppermute x9, starting transfers between devices, move(): return [lax.ppermute(p, 'chan', route) for p in parts]  26.6 us
    ppermute x9, waiting for transfers between devices, move(): return [lax.ppermute(p, 'chan', route) for p in parts]  14 us
    pallas_call x2, Pallas kernels, tiles(): pl.pallas_call(functools.partial(tile_kernel, distances, by_slot), out_sh...  10.3 us
    ppermute x7, starting transfers between devices, swap(): return [lax.ppermute(p, 'tm', [(0, 1), (1, 0)]) for p in parts]  9.57 us
    ppermute x7, waiting for transfers between devices, swap(): return [lax.ppermute(p, 'tm', [(0, 1), (1, 0)]) for p in parts]  2.85 us
    pallas_call x1, Pallas kernels, stack(): pl.pallas_call(stack_kernel, out_shape=[pltpu.VMEM((PAIRS * half, 2 * sam...  2.57 us
  transfers between devices with their start and end apart: 16, of which 8 were waited for; matrix products, arithmetic and copies ran while one was open for 3% of the time, Pallas kernels for 14%

profile of v4, /device:TPU:1, one launch (start us, length us, event | category | flops | bytes accessed | tf_op | source)
XLA Modules:
  0.0 69.7 jit_solution(14143387135412706774)
XLA Ops:
  0.0 7.7 %collective-permute-start = (bf16[128,1536]{1,0:T(8,128)(2,1)}, bf16[128,1536]{1,0:T(8,128)(2,1)S(1)}, u32[]{:S(2)}, u32[]{:S(2)}) collective-permute-start(bf16[128,1536]{1,0:T(8,128)(2,1)} %bitcast.9), channel_id=1, source_target_pairs={{16,0},{18,2},{20,4},{22,6},{24,8},{26,10},{28,12},{14,14},{32,16}... | collective-permute-start | bytes 1179656 | tf_op jit(solution)/shard_map/ppermute | solution.py:199
  7.7 1.7 %collective-permute-start.1 = (bf16[128,1536]{1,0:T(8,128)(2,1)}, bf16[128,1536]{1,0:T(8,128)(2,1)S(1)}, u32[]{:S(2)}, u32[]{:S(2)}) collective-permute-start(bf16[128,1536]{1,0:T(8,128)(2,1)} %bitcast.10), channel_id=1, source_target_pairs={{14,0},{0,2},{2,4},{4,6},{6,8},{8,10},{10,12},{12,14},{30,16},{16,... | collective-permute-start | bytes 1179656 | tf_op jit(solution)/shard_map/ppermute | solution.py:199
  9.4 3.3 %collective-permute-start.3 = (bf16[128,1536]{1,0:T(8,128)(2,1)}, bf16[128,1536]{1,0:T(8,128)(2,1)S(1)}, u32[]{:S(2)}, u32[]{:S(2)}) collective-permute-start(bf16[128,1536]{1,0:T(8,128)(2,1)} %bitcast.11), channel_id=1, source_target_pairs={{2,0},{4,2},{6,4},{8,6},{10,8},{12,10},{14,12},{16,14},{18,16},{20... | collective-permute-start | bytes 1179656 | tf_op jit(solution)/shard_map/ppermute | solution.py:199
  12.7 1.0 %dynamic-slice_bitcast_fusion = (bf16[64,1536]{1,0:T(8,128)(2,1)S(1)}, bf16[64,1536]{1,0:T(8,128)(2,1)S(1)}) fusion(bf16[1,1,128,1536]{3,2,1,0:T(8,128)(2,1)} %param.3, s32[]{:T(128)S(6)} %select_n.27, s32[]{:T(128)S(6)} %select_n.26), kind=kLoop, calls=%fused_computation.1 | loop fusion | bytes 786440 | tf_op jit(solution)/shard_map/dynamic_slice | solution.py:207
  13.7 1.0 %collective-permute-start.2 = (bf16[64,1536]{1,0:T(8,128)(2,1)S(1)}, bf16[64,1536]{1,0:T(8,128)(2,1)S(1)}, u32[]{:S(2)}, u32[]{:S(2)}) collective-permute-start(bf16[64,1536]{1,0:T(8,128)(2,1)S(1)} %get-tuple-element.34), channel_id=1, source_target_pairs={{0,1},{1,0},{2,3},{3,2},{4,5},{5,4},{6,7},{7,6},{8,9},{9,8},{10,11... | collective-permute-start | bytes 589832 | tf_op jit(solution)/shard_map/ppermute | solution.py:202
  14.8 1.1 %collective-permute-done.2.second = bf16[64,1536]{1,0:T(8,128)(2,1)S(1)} collective-permute-done((bf16[64,1536]{1,0:T(8,128)(2,1)S(1)}, bf16[64,1536]{1,0:T(8,128)(2,1)S(1)}, u32[]{:S(2)}, u32[]{:S(2)}) %collective-permute-start.2) | collective-permute-done | bytes 196640 | tf_op jit(solution)/shard_map/ppermute | solution.py:202
  15.9 3.0 %collective-permute-done.1 = bf16[128,1536]{1,0:T(8,128)(2,1)S(1)} collective-permute-done((bf16[128,1536]{1,0:T(8,128)(2,1)}, bf16[128,1536]{1,0:T(8,128)(2,1)S(1)}, u32[]{:S(2)}, u32[]{:S(2)}) %collective-permute-start.1) | collective-permute-done | bytes 393248 | tf_op jit(solution)/shard_map/ppermute | solution.py:199
  18.8 2.0 %collective-permute-done.3.refs_0_ = bf16[128,1536]{1,0:T(8,128)(2,1)S(1)} collective-permute-done((bf16[128,1536]{1,0:T(8,128)(2,1)}, bf16[128,1536]{1,0:T(8,128)(2,1)S(1)}, u32[]{:S(2)}, u32[]{:S(2)}) %collective-permute-start.3) | collective-permute-done | bytes 393248 | tf_op jit(solution)/shard_map/ppermute | solution.py:199
  21.7 0.7 compare_select_fusion.wanted
  22.3 1.3 %collective-permute-start.5 = (bf16[128,1536]{1,0:T(8,128)(2,1)S(1)}, bf16[128,1536]{1,0:T(8,128)(2,1)S(1)}, u32[]{:S(2)}, u32[]{:S(2)}) collective-permute-start(bf16[128,1536]{1,0:T(8,128)(2,1)S(1)} %collective-permute-done.3.refs_0_), channel_id=1, source_target_pairs={{2,0},{4,2},{6,4},{8,6},{10,8},{12,10},{14,12},{16,14},{18,16},{20... | collective-permute-start | bytes 1179656 | tf_op jit(solution)/shard_map/ppermute | solution.py:199
  23.6 2.6 %stack.1 = (bf16[1088,3200]{1,0:T(8,128)(2,1)S(1)}, f32[1,3,33,64,128]{4,3,2,1,0:T(8,128)}) custom-call(s32[3]{0:T(128)S(1)} %compare_select_fusion.wanted, bf16[64,1536]{1,0:T(8,128)(2,1)S(1)} %get-tuple-element.33.first, bf16[64,1536]{1,0:T(8,128)(2,1)S(1)} %collective-permute-done.2.second), custom_call_target="tpu_custom_call" | custom-call | tf_op jit(solution)/shard_map/stack/pallas_call | solution.py:54
  26.2 4.9 %collective-permute-done.4.refs_1_ = bf16[128,1536]{1,0:T(8,128)(2,1)S(1)} collective-permute-done((bf16[128,1536]{1,0:T(8,128)(2,1)S(1)}, bf16[128,1536]{1,0:T(8,128)(2,1)S(1)}, u32[]{:S(2)}, u32[]{:S(2)}) %collective-permute-start.4) | collective-permute-done | bytes 393248 | tf_op jit(solution)/shard_map/ppermute | solution.py:199
  31.2 3.2 %collective-permute-done.5.refs_2_ = bf16[128,1536]{1,0:T(8,128)(2,1)S(1)} collective-permute-done((bf16[128,1536]{1,0:T(8,128)(2,1)S(1)}, bf16[128,1536]{1,0:T(8,128)(2,1)S(1)}, u32[]{:S(2)}, u32[]{:S(2)}) %collective-permute-start.5) | collective-permute-done | bytes 393248 | tf_op jit(solution)/shard_map/ppermute | solution.py:199
  34.4 5.1 %collective-permute-start.6 = (bf16[128,1536]{1,0:T(8,128)(2,1)S(1)}, bf16[128,1536]{1,0:T(8,128)(2,1)S(1)}, u32[]{:S(2)}, u32[]{:S(2)}) collective-permute-start(bf16[128,1536]{1,0:T(8,128)(2,1)S(1)} %collective-permute-done.5.refs_2_), channel_id=1, source_target_pairs={{2,0},{4,2},{6,4},{8,6},{10,8},{12,10},{14,12},{16,14},{18,16},{20... | collective-permute-start | bytes 1179656 | tf_op jit(solution)/shard_map/ppermute | solution.py:199
  39.6 1.0 %collective-permute-done.7.refs_3_ = bf16[128,1536]{1,0:T(8,128)(2,1)S(1)} collective-permute-done((bf16[128,1536]{1,0:T(8,128)(2,1)S(1)}, bf16[128,1536]{1,0:T(8,128)(2,1)S(1)}, u32[]{:S(2)}, u32[]{:S(2)}) %collective-permute-start.7) | collective-permute-done | bytes 393248 | tf_op jit(solution)/shard_map/ppermute | solution.py:199
  40.5 1.1 %pick.1 = (bf16[128,1536]{1,0:T(8,128)(2,1)S(1)}, bf16[128,1536]{1,0:T(8,128)(2,1)S(1)}, bf16[128,1536]{1,0:T(8,128)(2,1)S(1)}) custom-call(s32[3]{0:T(128)S(1)} %compare_select_fusion.wanted, bf16[128,1536]{1,0:T(8,128)(2,1)S(1)} %collective-permute-done.3.refs_0_, bf16[128,1536]{1,0:T(8,128)(2,1)S(1)} %collective-permute-done.4.refs_1_, ...), custom_call_target="tpu_custom_call" | custom-call | tf_op jit(solution)/shard_map/pick/pallas_call | solution.py:110
  41.6 3.5 %collective-permute-start.10 = (bf16[128,1536]{1,0:T(8,128)(2,1)S(1)}, bf16[128,1536]{1,0:T(8,128)(2,1)S(1)}, u32[]{:S(2)}, u32[]{:S(2)}) collective-permute-start(bf16[128,1536]{1,0:T(8,128)(2,1)S(1)} %get-tuple-element.28.refs_1_), channel_id=1, source_target_pairs={{0,1},{1,0},{2,3},{3,2},{4,5},{5,4},{6,7},{7,6},{8,9},{9,8},{10,11... | collective-permute-start | bytes 1179656 | tf_op jit(solution)/shard_map/ppermute | solution.py:202
  45.6 7.2 %collective-permute-start.12 = (bf16[128,1536]{1,0:T(8,128)(2,1)S(1)}, bf16[128,1536]{1,0:T(8,128)(2,1)S(1)}, u32[]{:S(2)}, u32[]{:S(2)}) collective-permute-start(bf16[128,1536]{1,0:T(8,128)(2,1)S(1)} %collective-permute-done.6.refs_0_), channel_id=1, source_target_pairs={{2,0},{4,2},{6,4},{8,6},{10,8},{12,10},{14,12},{16,14},{18,16},{20... | collective-permute-start | bytes 1179656 | tf_op jit(solution)/shard_map/ppermute | solution.py:199
  52.9 4.0 %collective-permute-start.13 = (bf16[128,1536]{1,0:T(8,128)(2,1)S(1)}, bf16[128,1536]{1,0:T(8,128)(2,1)S(1)}, u32[]{:S(2)}, u32[]{:S(2)}) collective-permute-start(bf16[128,1536]{1,0:T(8,128)(2,1)S(1)} %collective-permute-done.6.refs_0_), channel_id=1, source_target_pairs={{0,1},{1,0},{2,3},{3,2},{4,5},{5,4},{6,7},{7,6},{8,9},{9,8},{10,11... | collective-permute-start | bytes 1179656 | tf_op jit(solution)/shard_map/ppermute | solution.py:202
  56.8 6.3 %tiles_1_7_2_6.1.refs_6_ = f32[1,3,33,64,128]{4,3,2,1,0:T(8,128)} custom-call(s32[3]{0:T(128)S(1)} %compare_select_fusion.wanted, bf16[1088,3200]{1,0:T(8,128)(2,1)S(1)} %get-tuple-element.23.rows, bf16[128,1536]{1,0:T(8,128)(2,1)S(1)} %get-tuple-element.27.refs_0_, bf16[128,1536]{1,0:T(8,128)(2,1)S(1)} %get-tuple-element.28.refs_1_, ...), custom_call_target="tpu_custom_call", output_to_operand_aliasing={{}: (8, {})} | custom-call | tf_op jit(solution)/shard_map/tiles_1_7_2_6/pallas_call | solution.py:166
  63.3 0.5 collective-permute-start.15
  63.8 1.2 %collective-permute-done.14.refs_4_ = bf16[128,1536]{1,0:T(8,128)(2,1)S(1)} collective-permute-done((bf16[128,1536]{1,0:T(8,128)(2,1)S(1)}, bf16[128,1536]{1,0:T(8,128)(2,1)S(1)}, u32[]{:S(2)}, u32[]{:S(2)}) %collective-permute-start.14) | collective-permute-done | bytes 393248 | tf_op jit(solution)/shard_map/ppermute | solution.py:202
  65.0 0.6 collective-permute-done.15.refs_5_
  65.5 4.0 %tiles_3_5_4.1 = f32[1,3,33,64,128]{4,3,2,1,0:T(8,128)} custom-call(s32[3]{0:T(128)S(1)} %compare_select_fusion.wanted, bf16[1088,3200]{1,0:T(8,128)(2,1)S(1)} %get-tuple-element.23.rows, bf16[128,1536]{1,0:T(8,128)(2,1)S(1)} %collective-permute-done.6.refs_0_, bf16[128,1536]{1,0:T(8,128)(2,1)S(1)} %collective-permute-done.8.refs_1_, ...), custom_call_target="tpu_custom_call", output_to_operand_aliasing={{}: (8, {})} | custom-call | tf_op jit(solution)/shard_map/tiles_3_5_4/pallas_call | solution.py:166
  (15 shorter events, 1.0 us)
Async XLA Ops:
  0.0 15.9 %collective-permute-start = (bf16[128,1536]{1,0:T(8,128)(2,1)}, bf16[128,1536]{1,0:T(8,128)(2,1)S(1)}, u32[]{:S(2)}, u32[]{:S(2)}) collective-permute-start(bf16[128,1536]{1,0:T(8,128)(2,1)} %bitcast.9), channel_id=1, source_target_pairs={{16,0},{18,2},{20,4},{22,6},{24,8},{26,10},{28,12},{14,14},{32,16}... | collective-permute-start | bytes 1179656 | tf_op jit(solution)/shard_map/ppermute | solution.py:199
  7.7 11.2 %collective-permute-start.1 = (bf16[128,1536]{1,0:T(8,128)(2,1)}, bf16[128,1536]{1,0:T(8,128)(2,1)S(1)}, u32[]{:S(2)}, u32[]{:S(2)}) collective-permute-start(bf16[128,1536]{1,0:T(8,128)(2,1)} %bitcast.10), channel_id=1, source_target_pairs={{14,0},{0,2},{2,4},{4,6},{6,8},{8,10},{10,12},{12,14},{30,16},{16,... | collective-permute-start | bytes 1179656 | tf_op jit(solution)/shard_map/ppermute | solution.py:199
  9.4 11.4 %collective-permute-start.3 = (bf16[128,1536]{1,0:T(8,128)(2,1)}, bf16[128,1536]{1,0:T(8,128)(2,1)S(1)}, u32[]{:S(2)}, u32[]{:S(2)}) collective-permute-start(bf16[128,1536]{1,0:T(8,128)(2,1)} %bitcast.11), channel_id=1, source_target_pairs={{2,0},{4,2},{6,4},{8,6},{10,8},{12,10},{14,12},{16,14},{18,16},{20... | collective-permute-start | bytes 1179656 | tf_op jit(solution)/shard_map/ppermute | solution.py:199
  13.7 2.1 %collective-permute-start.2 = (bf16[64,1536]{1,0:T(8,128)(2,1)S(1)}, bf16[64,1536]{1,0:T(8,128)(2,1)S(1)}, u32[]{:S(2)}, u32[]{:S(2)}) collective-permute-start(bf16[64,1536]{1,0:T(8,128)(2,1)S(1)} %get-tuple-element.34), channel_id=1, source_target_pairs={{0,1},{1,0},{2,3},{3,2},{4,5},{5,4},{6,7},{7,6},{8,9},{9,8},{10,11... | collective-permute-start | bytes 589832 | tf_op jit(solution)/shard_map/ppermute | solution.py:202
  20.8 10.3 %collective-permute-start.4 = (bf16[128,1536]{1,0:T(8,128)(2,1)S(1)}, bf16[128,1536]{1,0:T(8,128)(2,1)S(1)}, u32[]{:S(2)}, u32[]{:S(2)}) collective-permute-start(bf16[128,1536]{1,0:T(8,128)(2,1)S(1)} %collective-permute-done), channel_id=1, source_target_pairs={{14,0},{0,2},{2,4},{4,6},{6,8},{8,10},{10,12},{12,14},{30,16},{16,... | collective-permute-start | bytes 1179656 | tf_op jit(solution)/shard_map/ppermute | solution.py:199
  22.3 12.1 %collective-permute-start.5 = (bf16[128,1536]{1,0:T(8,128)(2,1)S(1)}, bf16[128,1536]{1,0:T(8,128)(2,1)S(1)}, u32[]{:S(2)}, u32[]{:S(2)}) collective-permute-start(bf16[128,1536]{1,0:T(8,128)(2,1)S(1)} %collective-permute-done.3.refs_0_), channel_id=1, source_target_pairs={{2,0},{4,2},{6,4},{8,6},{10,8},{12,10},{14,12},{16,14},{18,16},{20... | collective-permute-start | bytes 1179656 | tf_op jit(solution)/shard_map/ppermute | solution.py:199
  31.1 9.4 %collective-permute-start.7 = (bf16[128,1536]{1,0:T(8,128)(2,1)S(1)}, bf16[128,1536]{1,0:T(8,128)(2,1)S(1)}, u32[]{:S(2)}, u32[]{:S(2)}) collective-permute-start(bf16[128,1536]{1,0:T(8,128)(2,1)S(1)} %broadcast_select_fusion), channel_id=1, source_target_pairs={{14,0},{0,2},{2,4},{4,6},{6,8},{8,10},{10,12},{12,14},{30,16},{16,... | collective-permute-start | bytes 1179656 | tf_op jit(solution)/shard_map/ppermute | solution.py:199
  34.4 11.2 %collective-permute-start.6 = (bf16[128,1536]{1,0:T(8,128)(2,1)S(1)}, bf16[128,1536]{1,0:T(8,128)(2,1)S(1)}, u32[]{:S(2)}, u32[]{:S(2)}) collective-permute-start(bf16[128,1536]{1,0:T(8,128)(2,1)S(1)} %collective-permute-done.5.refs_2_), channel_id=1, source_target_pairs={{2,0},{4,2},{6,4},{8,6},{10,8},{12,10},{14,12},{16,14},{18,16},{20... | collective-permute-start | bytes 1179656 | tf_op jit(solution)/shard_map/ppermute | solution.py:199
  41.6 11.2 %collective-permute-start.10 = (bf16[128,1536]{1,0:T(8,128)(2,1)S(1)}, bf16[128,1536]{1,0:T(8,128)(2,1)S(1)}, u32[]{:S(2)}, u32[]{:S(2)}) collective-permute-start(bf16[128,1536]{1,0:T(8,128)(2,1)S(1)} %get-tuple-element.28.refs_1_), channel_id=1, source_target_pairs={{0,1},{1,0},{2,3},{3,2},{4,5},{5,4},{6,7},{7,6},{8,9},{9,8},{10,11... | collective-permute-start | bytes 1179656 | tf_op jit(solution)/shard_map/ppermute | solution.py:202
  45.1 11.7 %collective-permute-start.11 = (bf16[128,1536]{1,0:T(8,128)(2,1)S(1)}, bf16[128,1536]{1,0:T(8,128)(2,1)S(1)}, u32[]{:S(2)}, u32[]{:S(2)}) collective-permute-start(bf16[128,1536]{1,0:T(8,128)(2,1)S(1)} %get-tuple-element.29.refs_2_), channel_id=1, source_target_pairs={{0,1},{1,0},{2,3},{3,2},{4,5},{5,4},{6,7},{7,6},{8,9},{9,8},{10,11... | collective-permute-start | bytes 1179656 | tf_op jit(solution)/shard_map/ppermute | solution.py:202
  45.2 11.6 %collective-permute-start.9 = (bf16[128,1536]{1,0:T(8,128)(2,1)S(1)}, bf16[128,1536]{1,0:T(8,128)(2,1)S(1)}, u32[]{:S(2)}, u32[]{:S(2)}) collective-permute-start(bf16[128,1536]{1,0:T(8,128)(2,1)S(1)} %get-tuple-element.27.refs_0_), channel_id=1, source_target_pairs={{0,1},{1,0},{2,3},{3,2},{4,5},{5,4},{6,7},{7,6},{8,9},{9,8},{10,11... | collective-permute-start | bytes 1179656 | tf_op jit(solution)/shard_map/ppermute | solution.py:202
  45.6 17.6 %collective-permute-start.8 = (bf16[128,1536]{1,0:T(8,128)(2,1)S(1)}, bf16[128,1536]{1,0:T(8,128)(2,1)S(1)}, u32[]{:S(2)}, u32[]{:S(2)}) collective-permute-start(bf16[128,1536]{1,0:T(8,128)(2,1)S(1)} %collective-permute-done.7.refs_3_), channel_id=1, source_target_pairs={{254,0},{0,2},{2,4},{4,6},{6,8},{8,10},{10,12},{12,14},{14,16},{16... | collective-permute-start | bytes 1179656 | tf_op jit(solution)/shard_map/ppermute | solution.py:199
  45.6 17.7 %collective-permute-start.12 = (bf16[128,1536]{1,0:T(8,128)(2,1)S(1)}, bf16[128,1536]{1,0:T(8,128)(2,1)S(1)}, u32[]{:S(2)}, u32[]{:S(2)}) collective-permute-start(bf16[128,1536]{1,0:T(8,128)(2,1)S(1)} %collective-permute-done.6.refs_0_), channel_id=1, source_target_pairs={{2,0},{4,2},{6,4},{8,6},{10,8},{12,10},{14,12},{16,14},{18,16},{20... | collective-permute-start | bytes 1179656 | tf_op jit(solution)/shard_map/ppermute | solution.py:199
  52.9 10.9 %collective-permute-start.13 = (bf16[128,1536]{1,0:T(8,128)(2,1)S(1)}, bf16[128,1536]{1,0:T(8,128)(2,1)S(1)}, u32[]{:S(2)}, u32[]{:S(2)}) collective-permute-start(bf16[128,1536]{1,0:T(8,128)(2,1)S(1)} %collective-permute-done.6.refs_0_), channel_id=1, source_target_pairs={{0,1},{1,0},{2,3},{3,2},{4,5},{5,4},{6,7},{7,6},{8,9},{9,8},{10,11... | collective-permute-start | bytes 1179656 | tf_op jit(solution)/shard_map/ppermute | solution.py:202
  63.2 1.8 %collective-permute-start.14 = (bf16[128,1536]{1,0:T(8,128)(2,1)S(1)}, bf16[128,1536]{1,0:T(8,128)(2,1)S(1)}, u32[]{:S(2)}, u32[]{:S(2)}) collective-permute-start(bf16[128,1536]{1,0:T(8,128)(2,1)S(1)} %collective-permute-done.8.refs_1_), channel_id=1, source_target_pairs={{0,1},{1,0},{2,3},{3,2},{4,5},{5,4},{6,7},{7,6},{8,9},{9,8},{10,11... | collective-permute-start | bytes 1179656 | tf_op jit(solution)/shard_map/ppermute | solution.py:202
  63.3 2.3 %collective-permute-start.15 = (bf16[128,1536]{1,0:T(8,128)(2,1)S(1)}, bf16[128,1536]{1,0:T(8,128)(2,1)S(1)}, u32[]{:S(2)}, u32[]{:S(2)}) collective-permute-start(bf16[128,1536]{1,0:T(8,128)(2,1)S(1)} %collective-permute-done.12.refs_2_), channel_id=1, source_target_pairs={{0,1},{1,0},{2,3},{3,2},{4,5},{5,4},{6,7},{7,6},{8,9},{9,8},{10,11... | collective-permute-start | bytes 1179656 | tf_op jit(solution)/shard_map/ppermute | solution.py:202
